TPU v7x, 128 devices: a whole 4x4x4 slice. The times are simulated.
128 devices in a mesh: grp: 4 (over x_hi, core), tile: 32 (over x_lo, y, z).
Axes of the slice: x: 4 (x_hi: 2, x_lo: 2; x = x_hi * 2 + x_lo), y: 4, z: 4, core: 2. Of those that a mesh axis runs over, the one named last changes fastest.
Arguments:
- start_field: float32 [512, 512, 512], P('grp', 'tile'), may hold values from -4 to 4
- class_ids: int32 [512, 512], P('tile'), may hold values from 0 to 7
- run_levels: int32 [512, 8], replicated, may hold values from 0 to 7
- steepness: float32 [512], replicated, may hold values from 0.1 to 1
- step_pick: int32 [512], replicated, may hold values from 1 to 4
- input_layer: float32 [69, 2048], replicated, may hold values from -2 to 2
- output_layer: bfloat16 [2048, 262144], P(None, ('grp', 'tile')), may hold values from -0.125 to 0.125
- output_bias: float32 [262144], P(('grp', 'tile')), may hold values from -1.5 to 1.5
Outputs:
- misfit: bfloat16 [512, 262144], P(None, ('grp', 'tile'))
- output_next: bfloat16 [2048, 262144], P(None, ('grp', 'tile'))
- bias_next: float32 [262144], P(('grp', 'tile'))
- input_next: float32 [69, 2048], replicated
All inputs are finite; a program needn't handle non-finite values.
Results may differ from a plain program's by a relative error of at most 0.0029.
The roundings to bfloat16 on the way count: a program that leaves them out, or rounds other values in their place, can miss the bound.
Values sent between devices are 32-bit elements; how exact they have to be, the bound alone decides.
A program may use at most 128 MiB of HBM per device.

v0:
```python
import jax
import jax.numpy as jnp
from jax import lax
from jax.sharding import Mesh
from jax.sharding import PartitionSpec as P

STEPS = 4
LEVELS = 8
GRP = ("grp_0", "grp_1")
GRP_TILE = ("grp_0", "grp_1", "tile")


def with_halo(value, sides, width):
    for axis, dim in sides:
        size, length = (lax.axis_size(axis), value.shape[dim])
        up = [(i, (i + 1) % size) for i in range(size - 1)]
        down = [(j, i) for i, j in up]
        last = lax.slice_in_dim(value, length - width, length, axis=dim)
        initial = lax.slice_in_dim(value, 0, width, axis=dim)
        before = lax.ppermute(last, axis, up)
        after = lax.ppermute(initial, axis, down)
        value = jnp.concatenate([before, value, after], axis=dim)
    return value


def in_blocks(value, dim, length):
    shape = value.shape
    tiles = value.reshape(*shape[:dim], length, shape[dim] // length, *shape[dim + 1 :])
    return jnp.moveaxis(tiles, dim, 0)


def in_order(tiles, dim):
    tiles = jnp.moveaxis(tiles, 0, dim)
    shape = tiles.shape
    return tiles.reshape(*shape[:dim], shape[dim] * shape[dim + 1], *shape[dim + 2 :])


def turned_blocks(tiles, axes, order):
    inside = tiles.shape[1:]
    out = tiles.reshape(*(lax.axis_size(a) for a in axes), *inside)
    for k in order:
        out = lax.all_to_all(out, axes[k], k, k, tiled=True)
    return out.reshape(-1, *inside)


def core_and_chips(value, groups, order, split_dim, concat_dim):
    length = lax.axis_size(groups[0]) * lax.axis_size(groups[1])
    tiles = in_blocks(value, split_dim, length)
    return in_order(turned_blocks(tiles, groups, order), concat_dim)


def coefficients(run_levels, class_ids):
    table = 0.03 * jnp.exp(run_levels.astype(jnp.float32) * jnp.log(jnp.float32(1.35)))
    kappa = jnp.zeros((run_levels.shape[0],) + class_ids.shape, jnp.float32)
    for klass in range(run_levels.shape[1]):
        picked = jnp.where(class_ids == klass, 1.0, 0.0).astype(jnp.float32)
        kappa = kappa + picked[None] * table[:, klass][:, None, None]
    return kappa


def advance(field, kappa, steep):
    ratio = field * field
    spread = kappa * (1.0 + steep * ratio) / (1.0 + ratio)
    fpad = jnp.pad(field, ((0, 0), (0, 0), (1, 1)))
    spad = jnp.pad(spread, ((0, 0), (0, 0), (1, 1)))
    centre = field[:, 1:-1]
    middle = spread[:, 1:-1]
    total = centre + 0.5 * (middle + spread[:, :-2]) * (field[:, :-2] - centre)
    total = total + 0.5 * (middle + spread[:, 2:]) * (field[:, 2:] - centre)
    total = total + 0.5 * (middle + spad[:, 1:-1, :-2]) * (fpad[:, 1:-1, :-2] - centre)
    total = total + 0.5 * (middle + spad[:, 1:-1, 2:]) * (fpad[:, 1:-1, 2:] - centre)
    return total


def features(run_levels, step_pick, steepness):
    count = run_levels.shape[0]
    onehot = (run_levels[:, :, None] == jnp.arange(LEVELS, dtype=jnp.int32)[None, None, :]).astype(
        jnp.float32
    )
    onehot = onehot.reshape(count, -1)
    moment = (step_pick[:, None] == jnp.arange(1, STEPS + 1, dtype=jnp.int32)[None, :]).astype(
        jnp.float32
    )
    return jnp.concatenate([onehot, moment, steepness[:, None]], axis=1)


def dsilu(pre):
    logistic = jax.nn.sigmoid(pre)
    return logistic * (1.0 + pre * (1.0 - logistic))


def on_device(
    start_field, class_ids, run_levels, steepness, step_pick, input_layer, output_layer, output_bias
):
    local_runs, rows, columns = start_field.shape
    first_run = lax.axis_index(GRP) * local_runs
    levels_here = lax.dynamic_slice_in_dim(run_levels, first_run, local_runs, 0)
    steep = lax.dynamic_slice_in_dim(steepness, first_run, local_runs, 0)[:, None, None]
    pick_here = lax.dynamic_slice_in_dim(step_pick, first_run, local_runs, 0)[:, None, None]
    snapshot = jnp.zeros_like(start_field)
    class_wide = with_halo(class_ids + 1, (("tile", 0),), STEPS)
    kappa_wide = coefficients(levels_here, class_wide - 1)
    wide = with_halo(start_field, (("tile", 1),), STEPS)
    first_row = lax.axis_index("tile") * rows - STEPS
    total_rows = rows * lax.axis_size("tile")
    span = kappa_wide.shape[1]
    for step in range(STEPS):
        margin = STEPS - step - 1
        kappa_now = kappa_wide[:, step : span - step]
        wide = advance(wide, kappa_now, steep)
        row_ids = first_row + step + 1 + jnp.arange(wide.shape[1], dtype=jnp.int32)
        inside = (row_ids >= 0) & (row_ids < total_rows)
        wide = jnp.where(inside[None, :, None], wide, 0.0)
        snapshot = jnp.where(pick_here == step + 1, wide[:, margin : margin + rows], snapshot)
    flat = snapshot.reshape(local_runs, rows * columns)
    target = core_and_chips(flat, ("grp_0", "grp_1"), (0, 1), 1, 0)
    runs_total = target.shape[0]
    feats = features(run_levels, step_pick, steepness)
    pre = jnp.dot(feats, input_layer, precision=lax.Precision.HIGHEST)
    hidden = jax.nn.silu(pre).astype(jnp.bfloat16)
    error = (
        jnp.dot(hidden, output_layer, preferred_element_type=jnp.float32)
        + output_bias[None, :]
        - target
    )
    slope = (error * (2.0 / runs_total)).astype(jnp.bfloat16)
    grad = lax.dot_general(
        hidden, slope, (((0,), (0,)), ((), ())), preferred_element_type=jnp.float32
    )
    output_next = (output_layer.astype(jnp.float32) - 0.5 * grad).astype(jnp.bfloat16)
    bias_next = output_bias - 0.5 * jnp.sum(slope.astype(jnp.float32), axis=0)
    gain_slope = dsilu(pre)
    partial_back = lax.dot_general(
        slope, output_layer, (((1,), (1,)), ((), ())), preferred_element_type=jnp.float32
    )
    back = lax.psum(partial_back, GRP_TILE)
    grad_in = lax.dot_general(
        feats, back * gain_slope, (((0,), (0,)), ((), ())), precision=lax.Precision.HIGHEST
    )
    input_next = input_layer - 2.0 * grad_in
    return (error.astype(jnp.bfloat16), output_next, bias_next, input_next)


def solution(mesh):
    split = Mesh(mesh.devices.reshape(2, 2, mesh.shape["tile"]), ("grp_0", "grp_1", "tile"))
    return jax.shard_map(
        on_device,
        mesh=split,
        in_specs=(
            P(GRP, "tile", None),
            P("tile", None),
            P(),
            P(),
            P(),
            P(),
            P(None, GRP_TILE),
            P(GRP_TILE),
        ),
        out_specs=(P(None, GRP_TILE), P(None, GRP_TILE), P(GRP_TILE), P()),
        check_vma=False,
    )
```

profile of v0, /device:TPU:1, one launch (start us, length us, event | category | flops | bytes accessed | tf_op | source)
XLA Modules:
  0.0 393.0 jit_solution(14505002223111617005)
XLA Ops:
  7.2 0.0 copy-start.22
  7.2 0.8 broadcast_add_fusion
  8.0 4.4 %collective-permute-start.2 = (s32[4,512]{1,0:T(4,128)S(1)}, s32[4,512]{1,0:T(4,128)S(1)}, u32[]{:S(2)}, u32[]{:S(2)}) collective-permute-start(s32[4,512]{1,0:T(4,128)S(1)} %get-tuple-element.24), channel_id=1, source_target_pairs={{0,1},{1,2},{2,3},{3,4},{4,5},{5,6},{6,7},{7,8},{8,9},{9,10},{10,1... | collective-permute-start | bytes 24584 | tf_op jit(solution)/shard_map/ppermute | solution.py:20
  12.3 1.3 collective-permute-start.3
  13.6 2.7 fusion.96
  16.4 0.3 copy.34
  16.7 4.2 %collective-permute-start = (f32[128,4,512]{2,0,1:T(8,128)S(1)}, f32[128,4,512]{2,0,1:T(8,128)S(1)}, u32[]{:S(2)}, u32[]{:S(2)}) collective-permute-start(f32[128,4,512]{2,0,1:T(8,128)S(1)} %copy.34), channel_id=1, source_target_pairs={{0,1},{1,2},{2,3},{3,4},{4,5},{5,6},{6,7},{7,8},{8,9},{9,10},{10,1... | collective-permute-start | bytes 3145736 | tf_op jit(solution)/shard_map/ppermute | solution.py:20
  21.0 1.3 copy.35
  22.3 1.3 collective-permute-start.1
  23.6 0.0 copy-start.24
  23.7 0.6 compare_and_fusion.3
  24.3 0.6 compare_and_fusion
  24.8 0.6 compare_and_fusion.1
  25.4 1.3 broadcast_compare_fusion.3
  26.7 0.6 broadcast_compare_fusion.2
  27.3 0.6 compare_and_fusion.2
  27.8 5.3 %copy.29 = f32[128,16,512]{0,2,1:T(8,128)} copy(f32[128,16,512]{2,1,0:T(8,128)} %param.8) | data formatting | bytes 8388608 | tf_op args[0]
  33.1 0.8 dynamic_slice.11
  33.9 0.0 collective-permute-done.2
  33.9 0.0 collective-permute-done.3
  33.9 0.0 copy-start.8
  34.0 0.0 copy-start.10
  34.0 0.0 copy-start.12
  34.0 0.0 copy-start.14
  34.0 0.0 copy-start.16
  34.0 0.0 copy-start.18
  34.0 0.0 copy-start.20
  34.0 14.8 %multiply_add_fusion = f32[128,24,512]{0,2,1:T(8,128)} fusion(f32[128]{0:T(128)S(1)} %get-tuple-element.27, f32[24,512]{1,0:T(8,128)S(1)} %get-tuple-element.23, f32[128]{0:T(128)S(1)} %get-tuple-element.28, f32[24,512]{1,0:T(8,128)S(1)} %get-tuple-element.22, f32[128]{0:T(128)S(1)} %get-tuple-element.29, f32[24,512]{1,0:T(8,128)S(1)} %get-tuple-element.21, ...), kind=kLoop, calls=%fused_computation.3 | loop fusion | flops 23592960 | bytes 6688768 | tf_op jit(solution)/shard_map/add | solution.py:57
  48.8 0.0 copy-done.24
  49.0 0.0 collective-permute-done
  49.0 0.3 copy.28
  49.3 0.0 collective-permute-done.1
  49.3 1.5 copy.30
  50.9 0.0 copy-start.3
  50.9 1.0 copy-done.3
  51.9 0.0 copy-start.25
  52.0 2.7 pad_maximum_fusion
  54.7 0.6 copy-done.2
  55.4 15.7 %add_divide_fusion = f32[128,24,512]{0,2,1:T(8,128)S(1)} fusion(f32[128]{0:T(128)S(1)} %dynamic_slice.11, f32[128,4,512]{0,2,1:T(8,128)} %copy-done.3, f32[128,16,512]{0,2,1:T(8,128)S(1)} %copy-done.2, f32[128,4,512]{0,2,1:T(8,128)S(1)} %copy.28, f32[128]{0:T(128)S(1)} %copy-done.25, f32[24,512]{1,0:T(8,128)S(1)} %copy-done.9, f32[128]{0:T(128)S(1)} %copy-done.27, ...), kind=kLoop, calls=%fused_computation.2 | loop fusion | flops 36175872 | bytes 12980736 | tf_op jit(solution)/shard_map/div | solution.py:63
  71.1 11.3 %fusion.11 = (f32[128,22,512]{0,2,1:T(8,128)}, f32[128,22,512]{0,2,1:T(8,128)S(1)}) fusion(f32[128,24,512]{0,2,1:T(8,128)} %multiply_add_fusion, f32[128]{0:T(128)S(1)} %dynamic_slice.11, f32[128,24,512]{0,2,1:T(8,128)S(1)} %pad_maximum_fusion, f32[128,24,512]{0,2,1:T(8,128)S(1)} %add_divide_fusion, pred[22]{0:T(512)(128)(4,1)} %compare_and_fusion), kind=kLoop, calls=%fused_computation.20 | loop fusion | flops 38928384 | bytes 64487960 | tf_op jit(solution)/shard_map/div | solution.py:63
  82.4 16.6 %fusion.29 = (f32[128,20,512]{0,2,1:T(8,128)S(1)}, f32[128,20,512]{0,2,1:T(8,128)S(1)}) fusion(f32[128,24,512]{0,2,1:T(8,128)} %multiply_add_fusion, f32[128]{0:T(128)S(1)} %dynamic_slice.11, f32[128,22,512]{0,2,1:T(8,128)S(1)} %get-tuple-element.11, f32[128,22,512]{0,2,1:T(8,128)} %get-tuple-element.10, pred[20]{0:T(512)(128)(4,1)S(1)} %copy-done.46), kind=kLoop, calls=%fused_computation.47 | loop fusion | flops 35389440 | bytes 58721280 | tf_op jit(solution)/shard_map/div | solution.py:63
  99.1 10.9 %fusion.47 = (f32[128,18,512]{0,2,1:T(8,128)}, f32[128,18,512]{0,2,1:T(8,128)}) fusion(f32[128,24,512]{0,2,1:T(8,128)} %multiply_add_fusion, f32[128]{0:T(128)S(1)} %dynamic_slice.11, f32[128,20,512]{0,2,1:T(8,128)S(1)} %get-tuple-element.9, f32[128,20,512]{0,2,1:T(8,128)S(1)} %get-tuple-element.8, pred[18]{0:T(512)(128)(4,1)S(1)} %copy-done.45), kind=kLoop, calls=%fused_computation.74 | loop fusion | flops 31850496 | bytes 52954112 | tf_op jit(solution)/shard_map/div | solution.py:63
  110.0 21.7 %fusion.60 = f32[128,16,512]{0,2,1:T(8,128)} fusion(f32[128,18,512]{0,2,1:T(8,128)} %get-tuple-element.6, f32[128,18,512]{0,2,1:T(8,128)} %get-tuple-element.7, f32[128,22,512]{0,2,1:T(8,128)} %copy-done, f32[128,20,512]{0,2,1:T(8,128)} %copy-done.1, pred[16]{0:T(512)(128)(4,1)S(1)} %copy-done.44, pred[128]{0:T(512)(128)(4,1)S(1)} %copy-done.43, ...), kind=kLoop, calls=%fused_computation.95 | loop fusion | flops 26214400 | bytes 47186448 | tf_op jit(solution)/shard_map/jit(_where)/select_n | solution.py:114
  131.7 5.6 %copy.31 = f32[4,128,2048]{2,1,0:T(8,128)} copy(f32[4,128,2048]{1,2,0:T(8,128)} %bitcast.30) | data formatting | bytes 8388608 | tf_op jit(solution)/shard_map/transpose | solution.py:29
  137.3 5.8 %all-to-all-start = ((f32[2,2,128,2048]{3,2,1,0:T(8,128)}), f32[2,2,128,2048]{3,2,1,0:T(8,128)}, u32[]{:S(2)}, u32[]{:S(2)}) async-start(f32[2,2,128,2048]{3,2,1,0:T(8,128)} %bitcast.31), calls=%async_computation | async-start | bytes 8388608 | tf_op jit(solution)/shard_map/all_to_all | solution.py:42
  143.0 0.0 all-reduce.10.cloned.1.call-start
  143.1 0.1 eq.141
  143.2 0.1 compare_convert_fusion
  143.3 0.1 fusion.87
  143.4 5.1 %fusion.88 = f32[512,2048]{1,0:T(8,128)} fusion(f32[69,2048]{1,0:T(8,128)S(1)} %copy-done.5, f32[512,1]{0,1:T(1,128)S(1)} %bitcast.32, f32[512,4]{0,1:T(4,128)S(1)} %compare_convert_fusion, f32[512,64]{0,1:T(8,128)S(1)} %fusion.87), kind=kOutput, calls=%fused_computation.131 | convolution fusion | flops 868291584 | bytes 4900864 | tf_op jit(solution)/shard_map/dot_general | solution.py:119
  148.5 42.2 %all-to-all-done = f32[2,2,128,2048]{3,2,1,0:T(8,128)} async-done(((f32[2,2,128,2048]{3,2,1,0:T(8,128)}), f32[2,2,128,2048]{3,2,1,0:T(8,128)}, u32[]{:S(2)}, u32[]{:S(2)}) %all-to-all-start) | async-done | bytes 4194336 | tf_op jit(solution)/shard_map/all_to_all | solution.py:42
  190.6 2.6 copy.32
  193.2 0.0 slice-start.1
  193.3 9.2 %all_to_all.10 = f32[2,2,128,2048]{3,2,0,1:T(8,128)S(1)} all-to-all(f32[2,2,128,2048]{3,2,0,1:T(8,128)S(1)} %copy.32), channel_id=1, replica_groups=mesh['grp_0'=2,'grp_1'=2,'tile'=32] {'grp_1'}, dimensions={1} | all-to-all | bytes 8388608 | tf_op jit(solution)/shard_map/all_to_all | solution.py:42
  202.5 0.5 copy.33
  203.0 1.7 copy-done.4
  204.7 6.1 %convert_reduce_fusion = (f32[2048]{0:T(1024)S(1)}, bf16[512,2048]{1,0:T(8,128)(2,1)}, f32[512,2048]{1,0:T(8,128)S(1)}) fusion(f32[2,2,128,2048]{3,2,1,0:T(8,128)S(1)} %copy.33, f32[2048]{0:T(1024)S(1)} %copy-done.23, bf16[2048,2048]{1,0:T(8,128)(2,1)S(1)} %bitcast.35, f32[512,2048]{1,0:T(8,128)S(1)} %copy-done.4), kind=kOutput, calls=%fused_computation.121 | convolution fusion | flops 4307548160 | bytes 23085056 | tf_op jit(solution)/shard_map/dot_general | solution.py:122
  210.7 2.1 copy-done.47
  212.8 6.2 %fusion.92 = f32[512,2048]{1,0:T(8,128)} fusion(bf16[2048,2048]{1,0:T(8,128)(2,1)S(1)} %bitcast.35, f32[512,2048]{1,0:T(8,128)S(1)} %get-tuple-element.37), kind=kOutput, calls=%fused_computation.165 | convolution fusion | flops 4297064448 | bytes 16777216 | tf_op jit(solution)/shard_map/dot_general | solution.py:133
  219.0 0.0 all-reduce.10.cloned.1.call-update
  219.0 0.6 multiply_subtract_fusion
  219.6 14.6 %subtract_convert_fusion = bf16[2048,2048]{1,0:T(8,128)(2,1)} fusion(bf16[2048,2048]{1,0:T(8,128)(2,1)} %param.14, f32[512,2048]{1,0:T(8,128)} %copy-done.47, f32[512,2048]{1,0:T(8,128)} %fusion.88), kind=kOutput, calls=%fused_computation | convolution fusion | flops 4319084544 | bytes 25165824 | tf_op jit(solution)/shard_map/dot_general | solution.py:127
  234.2 143.7 %all-reduce.10.cloned.1.call-done = f32[512,2048]{1,0:T(8,128)} async-done(((f32[512,2048]{1,0:T(8,128)}), f32[512,2048]{1,0:T(8,128)}) %all-reduce.10.cloned.1.call-update) | async-done | bytes 4194320 | tf_op jit(solution)/shard_map/psum | solution.py:136
  377.9 8.2 %fusion.83 = f32[69,2048]{1,0:T(8,128)} fusion(f32[69,2048]{1,0:T(8,128)S(1)} %copy-done.5, f32[512,2048]{1,0:T(8,128)} %all-reduce.10.cloned.1.call-done, f32[512,2048]{1,0:T(8,128)} %fusion.88, f32[512,1]{0,1:T(1,128)S(1)} %bitcast.33, f32[512,4]{0,1:T(4,128)S(1)} %compare_convert_fusion, f32[512,64]{0,1:T(8,128)S(1)} %fusion.87), kind=kOutput, calls=%fused_computation.126 | convolution fusion | flops 876962816 | bytes 9660416 | tf_op jit(solution)/shard_map/dot_general | solution.py:137
  (91 shorter events, 0.3 us)
Async XLA Ops:
  7.2 16.4 %copy-start.22 = (s32[512,8]{0,1:T(8,128)S(1)}, s32[512,8]{0,1:T(8,128)}, u32[]{:S(2)}) copy-start(s32[512,8]{0,1:T(8,128)} %param.10) | copy-start | bytes 49156
  8.0 25.9 %collective-permute-start.2 = (s32[4,512]{1,0:T(4,128)S(1)}, s32[4,512]{1,0:T(4,128)S(1)}, u32[]{:S(2)}, u32[]{:S(2)}) collective-permute-start(s32[4,512]{1,0:T(4,128)S(1)} %get-tuple-element.24), channel_id=1, source_target_pairs={{0,1},{1,2},{2,3},{3,4},{4,5},{5,6},{6,7},{7,8},{8,9},{9,10},{10,1... | collective-permute-start | bytes 24584 | tf_op jit(solution)/shard_map/ppermute | solution.py:20
  12.3 21.6 %collective-permute-start.3 = (s32[4,512]{1,0:T(4,128)S(1)}, s32[4,512]{1,0:T(4,128)S(1)}, u32[]{:S(2)}, u32[]{:S(2)}) collective-permute-start(s32[4,512]{1,0:T(4,128)S(1)} %get-tuple-element.25), channel_id=1, source_target_pairs={{1,0},{2,1},{3,2},{4,3},{5,4},{6,5},{7,6},{8,7},{9,8},{10,9},{11,1... | collective-permute-start | bytes 24584 | tf_op jit(solution)/shard_map/ppermute | solution.py:21
  16.7 32.2 %collective-permute-start = (f32[128,4,512]{2,0,1:T(8,128)S(1)}, f32[128,4,512]{2,0,1:T(8,128)S(1)}, u32[]{:S(2)}, u32[]{:S(2)}) collective-permute-start(f32[128,4,512]{2,0,1:T(8,128)S(1)} %copy.34), channel_id=1, source_target_pairs={{0,1},{1,2},{2,3},{3,4},{4,5},{5,6},{6,7},{7,8},{8,9},{9,10},{10,1... | collective-permute-start | bytes 3145736 | tf_op jit(solution)/shard_map/ppermute | solution.py:20
  22.3 27.0 %collective-permute-start.1 = (f32[128,4,512]{2,0,1:T(8,128)}, f32[128,4,512]{2,0,1:T(8,128)}, u32[]{:S(2)}, u32[]{:S(2)}) collective-permute-start(f32[128,4,512]{2,0,1:T(8,128)} %copy.35), channel_id=1, source_target_pairs={{1,0},{2,1},{3,2},{4,3},{5,4},{6,5},{7,6},{8,7},{9,8},{10,9},{11,1... | collective-permute-start | bytes 3145736 | tf_op jit(solution)/shard_map/ppermute | solution.py:21
  23.6 25.2 %copy-start.24 = (f32[128]{0:T(128)}, f32[128]{0:T(128)S(1)}, u32[]{:S(2)}) copy-start(f32[128]{0:T(128)S(1)} %get-tuple-element.27) | copy-start | bytes 1540
  23.6 25.2 %copy-start.26 = (f32[128]{0:T(128)}, f32[128]{0:T(128)S(1)}, u32[]{:S(2)}) copy-start(f32[128]{0:T(128)S(1)} %get-tuple-element.28) | copy-start | bytes 1540
  23.6 25.2 %copy-start.28 = (f32[128]{0:T(128)}, f32[128]{0:T(128)S(1)}, u32[]{:S(2)}) copy-start(f32[128]{0:T(128)S(1)} %get-tuple-element.29) | copy-start | bytes 1540
  23.6 25.2 %copy-start.30 = (f32[128]{0:T(128)}, f32[128]{0:T(128)S(1)}, u32[]{:S(2)}) copy-start(f32[128]{0:T(128)S(1)} %get-tuple-element.30) | copy-start | bytes 1540
  23.6 25.2 %copy-start.32 = (f32[128]{0:T(128)}, f32[128]{0:T(128)S(1)}, u32[]{:S(2)}) copy-start(f32[128]{0:T(128)S(1)} %get-tuple-element.31) | copy-start | bytes 1540
  23.7 25.2 %copy-start.34 = (f32[128]{0:T(128)}, f32[128]{0:T(128)S(1)}, u32[]{:S(2)}) copy-start(f32[128]{0:T(128)S(1)} %get-tuple-element.32) | copy-start | bytes 1540
  23.7 25.2 %copy-start.36 = (f32[128]{0:T(128)}, f32[128]{0:T(128)S(1)}, u32[]{:S(2)}) copy-start(f32[128]{0:T(128)S(1)} %get-tuple-element.33) | copy-start | bytes 1540
  33.9 15.0 %copy-start.6 = (f32[24,512]{1,0:T(8,128)}, f32[24,512]{1,0:T(8,128)S(1)}, u32[]{:S(2)}) copy-start(f32[24,512]{1,0:T(8,128)S(1)} %get-tuple-element.22) | copy-start | bytes 147460
  33.9 15.0 %copy-start.8 = (f32[24,512]{1,0:T(8,128)}, f32[24,512]{1,0:T(8,128)S(1)}, u32[]{:S(2)}) copy-start(f32[24,512]{1,0:T(8,128)S(1)} %get-tuple-element.23) | copy-start | bytes 147460
  34.0 14.9 %copy-start.10 = (f32[24,512]{1,0:T(8,128)}, f32[24,512]{1,0:T(8,128)S(1)}, u32[]{:S(2)}) copy-start(f32[24,512]{1,0:T(8,128)S(1)} %get-tuple-element.16) | copy-start | bytes 147460
  34.0 14.9 %copy-start.12 = (f32[24,512]{1,0:T(8,128)}, f32[24,512]{1,0:T(8,128)S(1)}, u32[]{:S(2)}) copy-start(f32[24,512]{1,0:T(8,128)S(1)} %get-tuple-element.17) | copy-start | bytes 147460
  34.0 14.9 %copy-start.14 = (f32[24,512]{1,0:T(8,128)}, f32[24,512]{1,0:T(8,128)S(1)}, u32[]{:S(2)}) copy-start(f32[24,512]{1,0:T(8,128)S(1)} %get-tuple-element.18) | copy-start | bytes 147460
  34.0 14.9 %copy-start.16 = (f32[24,512]{1,0:T(8,128)}, f32[24,512]{1,0:T(8,128)S(1)}, u32[]{:S(2)}) copy-start(f32[24,512]{1,0:T(8,128)S(1)} %get-tuple-element.19) | copy-start | bytes 147460
  34.0 14.9 %copy-start.18 = (f32[24,512]{1,0:T(8,128)}, f32[24,512]{1,0:T(8,128)S(1)}, u32[]{:S(2)}) copy-start(f32[24,512]{1,0:T(8,128)S(1)} %get-tuple-element.20) | copy-start | bytes 147460
  34.0 14.9 %copy-start.20 = (f32[24,512]{1,0:T(8,128)}, f32[24,512]{1,0:T(8,128)S(1)}, u32[]{:S(2)}) copy-start(f32[24,512]{1,0:T(8,128)S(1)} %get-tuple-element.21) | copy-start | bytes 147460
  50.9 1.0 copy-start.3
  51.9 3.4 copy-start.2
  51.9 3.4 copy-start.7
  51.9 3.5 copy-start.9
  51.9 3.5 copy-start.11
  51.9 3.4 copy-start.13
  51.9 3.4 copy-start.15
  51.9 3.4 copy-start.17
  51.9 3.4 copy-start.19
  51.9 3.4 copy-start.21
  51.9 3.4 copy-start.25
  51.9 3.4 copy-start.27
  51.9 3.4 copy-start.29
  51.9 3.4 copy-start.31
  52.0 3.4 copy-start.33
  52.0 3.4 copy-start.35
  52.0 3.4 copy-start.37
  71.1 11.3 %copy-start.46 = (pred[20]{0:T(512)(128)(4,1)S(1)}, pred[20]{0:T(512)(128)(4,1)}, u32[]{:S(2)}) copy-start(pred[20]{0:T(512)(128)(4,1)} %compare_and_fusion.1) | copy-start | bytes 64
  82.4 16.6 %copy-start = (f32[128,22,512]{0,2,1:T(8,128)}, f32[128,22,512]{0,2,1:T(8,128)S(1)}, u32[]{:S(2)}) copy-start(f32[128,22,512]{0,2,1:T(8,128)S(1)} %get-tuple-element.11) | copy-start | bytes 17301508
  82.4 16.7 %copy-start.45 = (pred[18]{0:T(512)(128)(4,1)S(1)}, pred[18]{0:T(512)(128)(4,1)}, u32[]{:S(2)}) copy-start(pred[18]{0:T(512)(128)(4,1)} %compare_and_fusion.2) | copy-start | bytes 58
  99.0 10.9 %copy-start.1 = (f32[128,20,512]{0,2,1:T(8,128)}, f32[128,20,512]{0,2,1:T(8,128)S(1)}, u32[]{:S(2)}) copy-start(f32[128,20,512]{0,2,1:T(8,128)S(1)} %get-tuple-element.9) | copy-start | bytes 15728644
  99.0 10.9 %copy-start.40 = (pred[128]{0:T(512)(128)(4,1)S(1)}, pred[128]{0:T(512)(128)(4,1)}, u32[]{:S(2)}) copy-start(pred[128]{0:T(512)(128)(4,1)} %get-tuple-element.4) | copy-start | bytes 388
  99.0 10.9 %copy-start.41 = (pred[128]{0:T(512)(128)(4,1)S(1)}, pred[128]{0:T(512)(128)(4,1)}, u32[]{:S(2)}) copy-start(pred[128]{0:T(512)(128)(4,1)} %get-tuple-element.34) | copy-start | bytes 388
  99.0 10.9 %copy-start.42 = (pred[128]{0:T(512)(128)(4,1)S(1)}, pred[128]{0:T(512)(128)(4,1)}, u32[]{:S(2)}) copy-start(pred[128]{0:T(512)(128)(4,1)} %get-tuple-element.35) | copy-start | bytes 388
  99.1 10.9 %copy-start.43 = (pred[128]{0:T(512)(128)(4,1)S(1)}, pred[128]{0:T(512)(128)(4,1)}, u32[]{:S(2)}) copy-start(pred[128]{0:T(512)(128)(4,1)} %get-tuple-element.36) | copy-start | bytes 388
  99.1 10.9 %copy-start.44 = (pred[16]{0:T(512)(128)(4,1)S(1)}, pred[16]{0:T(512)(128)(4,1)}, u32[]{:S(2)}) copy-start(pred[16]{0:T(512)(128)(4,1)} %compare_and_fusion.3) | copy-start | bytes 52
  137.3 5.9 %copy-start.38 = (s32[512]{0:T(512)S(1)}, s32[512]{0:T(512)}, u32[]{:S(2)}) copy-start(s32[512]{0:T(512)} %param.12) | copy-start | bytes 6148
  137.3 6.1 %copy-start.5 = (f32[69,2048]{1,0:T(8,128)S(1)}, f32[69,2048]{1,0:T(8,128)}, u32[]{:S(2)}) copy-start(f32[69,2048]{1,0:T(8,128)} %param.13) | copy-start | bytes 1695748
  137.3 6.1 %copy-start.39 = (f32[512]{0:T(512)S(1)}, f32[512]{0:T(512)}, u32[]{:S(2)}) copy-start(f32[512]{0:T(512)} %param.11) | copy-start | bytes 6148
  137.3 53.4 %all-to-all-start = ((f32[2,2,128,2048]{3,2,1,0:T(8,128)}), f32[2,2,128,2048]{3,2,1,0:T(8,128)}, u32[]{:S(2)}, u32[]{:S(2)}) async-start(f32[2,2,128,2048]{3,2,1,0:T(8,128)} %bitcast.31), calls=%async_computation | async-start | bytes 8388608 | tf_op jit(solution)/shard_map/all_to_all | solution.py:42
  143.0 234.9 %all-reduce.10.cloned.1.call-start = ((), (), s32[]{:S(2)}) async-start(), calls=%async_computation.2 | async-start | bytes 8388608 | tf_op jit(solution)/shard_map/psum | solution.py:136
  190.6 12.4 %slice-start = ((s8[8388608]{0:T(1024)(128)(4,1)}), s8[4194304]{0:T(1024)(128)(4,1)S(1)}, s32[]{:S(2)}) async-start(s8[8388608]{0:T(1024)(128)(4,1)} %bitcast.34), calls=%async_computation.3 | async-start | bytes 8388608
  193.2 9.8 %slice-start.1 = ((s8[8388608]{0:T(1024)(128)(4,1)}), s8[4194304]{0:T(1024)(128)(4,1)S(1)}, s32[]{:S(2)}) async-start(s8[8388608]{0:T(1024)(128)(4,1)} %bitcast.34), calls=%async_computation.4 | async-start | bytes 8388608
  202.5 2.2 copy-start.4
  202.5 2.2 copy-start.23
  210.7 2.1 copy-start.47
Sparse Core Ops, SparseCore 0:
  219.1 158.7 all-reduce.9
where the time goes:
time: 394 us; the launch traced here: 393 us
  waiting for transfers between devices  186 us (47%)
  other arithmetic  99.4 us (25%)
  matrix products  40.2 us (10%)
  local copies, waits for them, and re-layouts  26.5 us (7%)
  starting transfers between devices  17 us (4%)
  between operations  14.8 us (4%)
  blocking collectives  9.24 us (2%)
    psum x1, waiting for transfers between devices, on_device(): back = lax.psum(partial_back, GRP_TILE)  144 us
    div x4, other arithmetic, advance(): spread = kappa * (1.0 + steep * ratio) / (1.0 + ratio)  54.4 us
    all_to_all x1, waiting for transfers between devices, turned_blocks(): out = lax.all_to_all(out, axes[k], k, k, tiled=True)  42.2 us
    select_n x1, other arithmetic, on_device(): jnp.where(pick_here == step + 1, wide[:, margin:margin + rows], snapshot)  21.7 us
    add x1, other arithmetic, coefficients(): kappa = kappa + picked[None] * table[:, klass][:, None, None]  14.8 us
    dot_general x1, matrix products, on_device(): lax.dot_general(hidden, slope, (((0,), (0,)), ((), ())), preferred_elemen...  14.6 us
    unnamed x103, local copies, waits for them, and re-layouts  12.4 us
    all_to_all x1, blocking collectives, turned_blocks(): out = lax.all_to_all(out, axes[k], k, k, tiled=True)  9.24 us
  transfers between devices with their start and end apart: 6, of which 2 were waited for; matrix products, arithmetic and copies ran while one was open for 13% of the time, Pallas kernels for 0%

commit v1 on v0

--- a/solution.py
+++ b/solution.py
@@ -133,10 +133,10 @@
     partial_back = lax.dot_general(
         slope, output_layer, (((1,), (1,)), ((), ())), preferred_element_type=jnp.float32
     )
-    back = lax.psum(partial_back, GRP_TILE)
-    grad_in = lax.dot_general(
-        feats, back * gain_slope, (((0,), (0,)), ((), ())), precision=lax.Precision.HIGHEST
+    partial_in = lax.dot_general(
+        feats, partial_back * gain_slope, (((0,), (0,)), ((), ())), precision=lax.Precision.HIGHEST
     )
+    grad_in = lax.psum(partial_in, GRP_TILE)
     input_next = input_layer - 2.0 * grad_in
     return (error.astype(jnp.bfloat16), output_next, bias_next, input_next)
 

time: 394 us -> 384 us (0.975)
  waiting for transfers between devices: 186 us -> 177 us
    psum x1, waiting for transfers between devices: 144 us -> 135 us  [on_device(): grad_in = lax.psum(partial_in, GRP_TILE)]
where the time goes in v1:
time: 384 us; the launch traced here: 383 us
  waiting for transfers between devices  177 us (46%)
  other arithmetic  101 us (26%)
  matrix products  38.8 us (10%)
  local copies, waits for them, and re-layouts  24.5 us (6%)
  starting transfers between devices  17 us (4%)
  between operations  14.8 us (4%)
  blocking collectives  9.24 us (2%)
    psum x1, waiting for transfers between devices, on_device(): grad_in = lax.psum(partial_in, GRP_TILE)  135 us
    div x4, other arithmetic, advance(): spread = kappa * (1.0 + steep * ratio) / (1.0 + ratio)  54.4 us
    all_to_all x1, waiting for transfers between devices, turned_blocks(): out = lax.all_to_all(out, axes[k], k, k, tiled=True)  42.2 us
    select_n x1, other arithmetic, on_device(): jnp.where(pick_here == step + 1, wide[:, margin:margin + rows], snapshot)  21.7 us
    add x1, other arithmetic, coefficients(): kappa = kappa + picked[None] * table[:, klass][:, None, None]  14.8 us
    dot_general x1, matrix products, on_device(): lax.dot_general(hidden, slope, (((0,), (0,)), ((), ())), preferred_elemen...  14.6 us
    unnamed x103, local copies, waits for them, and re-layouts  10.4 us
    all_to_all x1, blocking collectives, turned_blocks(): out = lax.all_to_all(out, axes[k], k, k, tiled=True)  9.24 us
  transfers between devices with their start and end apart: 6, of which 2 were waited for; matrix products, arithmetic and copies ran while one was open for 13% of the time, Pallas kernels for 0%

profile of v1, /device:TPU:1, one launch (start us, length us, event | category | flops | bytes accessed | tf_op | source)
XLA Modules:
  0.0 382.8 jit_solution(13823181372475220173)
XLA Ops:
  7.2 0.0 copy-start.22
  7.2 0.8 broadcast_add_fusion
  8.0 4.4 %collective-permute-start.2 = (s32[4,512]{1,0:T(4,128)S(1)}, s32[4,512]{1,0:T(4,128)S(1)}, u32[]{:S(2)}, u32[]{:S(2)}) collective-permute-start(s32[4,512]{1,0:T(4,128)S(1)} %get-tuple-element.24), channel_id=1, source_target_pairs={{0,1},{1,2},{2,3},{3,4},{4,5},{5,6},{6,7},{7,8},{8,9},{9,10},{10,1... | collective-permute-start | bytes 24584 | tf_op jit(solution)/shard_map/ppermute | solution.py:20
  12.3 1.3 collective-permute-start.3
  13.6 2.7 fusion.90
  16.4 0.3 copy.34
  16.7 4.2 %collective-permute-start = (f32[128,4,512]{2,0,1:T(8,128)S(1)}, f32[128,4,512]{2,0,1:T(8,128)S(1)}, u32[]{:S(2)}, u32[]{:S(2)}) collective-permute-start(f32[128,4,512]{2,0,1:T(8,128)S(1)} %copy.34), channel_id=1, source_target_pairs={{0,1},{1,2},{2,3},{3,4},{4,5},{5,6},{6,7},{7,8},{8,9},{9,10},{10,1... | collective-permute-start | bytes 3145736 | tf_op jit(solution)/shard_map/ppermute | solution.py:20
  21.0 1.3 copy.35
  22.3 1.3 collective-permute-start.1
  23.6 0.0 copy-start.24
  23.7 0.6 compare_and_fusion.3
  24.3 0.6 compare_and_fusion
  24.8 0.6 compare_and_fusion.1
  25.4 1.3 broadcast_compare_fusion.3
  26.7 0.6 broadcast_compare_fusion.2
  27.3 0.6 compare_and_fusion.2
  27.8 5.3 %copy.29 = f32[128,16,512]{0,2,1:T(8,128)} copy(f32[128,16,512]{2,1,0:T(8,128)} %param.8) | data formatting | bytes 8388608 | tf_op args[0]
  33.1 0.8 dynamic_slice.11
  33.9 0.0 collective-permute-done.2
  33.9 0.0 collective-permute-done.3
  33.9 0.0 copy-start.8
  34.0 0.0 copy-start.10
  34.0 0.0 copy-start.12
  34.0 0.0 copy-start.14
  34.0 0.0 copy-start.16
  34.0 0.0 copy-start.18
  34.0 0.0 copy-start.20
  34.0 14.8 %multiply_add_fusion = f32[128,24,512]{0,2,1:T(8,128)} fusion(f32[128]{0:T(128)S(1)} %get-tuple-element.27, f32[24,512]{1,0:T(8,128)S(1)} %get-tuple-element.23, f32[128]{0:T(128)S(1)} %get-tuple-element.28, f32[24,512]{1,0:T(8,128)S(1)} %get-tuple-element.22, f32[128]{0:T(128)S(1)} %get-tuple-element.29, f32[24,512]{1,0:T(8,128)S(1)} %get-tuple-element.21, ...), kind=kLoop, calls=%fused_computation.3 | loop fusion | flops 23592960 | bytes 6688768 | tf_op jit(solution)/shard_map/add | solution.py:57
  48.8 0.0 copy-done.24
  49.0 0.0 collective-permute-done
  49.0 0.3 copy.28
  49.3 0.0 collective-permute-done.1
  49.3 1.5 copy.30
  50.9 0.0 copy-start.3
  50.9 1.0 copy-done.3
  51.9 0.0 copy-start.25
  52.0 2.7 pad_maximum_fusion
  54.7 0.6 copy-done.2
  55.4 15.7 %add_divide_fusion = f32[128,24,512]{0,2,1:T(8,128)S(1)} fusion(f32[128]{0:T(128)S(1)} %dynamic_slice.11, f32[128,4,512]{0,2,1:T(8,128)} %copy-done.3, f32[128,16,512]{0,2,1:T(8,128)S(1)} %copy-done.2, f32[128,4,512]{0,2,1:T(8,128)S(1)} %copy.28, f32[128]{0:T(128)S(1)} %copy-done.25, f32[24,512]{1,0:T(8,128)S(1)} %copy-done.9, f32[128]{0:T(128)S(1)} %copy-done.27, ...), kind=kLoop, calls=%fused_computation.2 | loop fusion | flops 36175872 | bytes 12980736 | tf_op jit(solution)/shard_map/div | solution.py:63
  71.1 11.3 %fusion.11 = (f32[128,22,512]{0,2,1:T(8,128)}, f32[128,22,512]{0,2,1:T(8,128)S(1)}) fusion(f32[128,24,512]{0,2,1:T(8,128)} %multiply_add_fusion, f32[128]{0:T(128)S(1)} %dynamic_slice.11, f32[128,24,512]{0,2,1:T(8,128)S(1)} %pad_maximum_fusion, f32[128,24,512]{0,2,1:T(8,128)S(1)} %add_divide_fusion, pred[22]{0:T(512)(128)(4,1)} %compare_and_fusion), kind=kLoop, calls=%fused_computation.20 | loop fusion | flops 38928384 | bytes 64487960 | tf_op jit(solution)/shard_map/div | solution.py:63
  82.4 16.6 %fusion.29 = (f32[128,20,512]{0,2,1:T(8,128)S(1)}, f32[128,20,512]{0,2,1:T(8,128)S(1)}) fusion(f32[128,24,512]{0,2,1:T(8,128)} %multiply_add_fusion, f32[128]{0:T(128)S(1)} %dynamic_slice.11, f32[128,22,512]{0,2,1:T(8,128)S(1)} %get-tuple-element.11, f32[128,22,512]{0,2,1:T(8,128)} %get-tuple-element.10, pred[20]{0:T(512)(128)(4,1)S(1)} %copy-done.46), kind=kLoop, calls=%fused_computation.47 | loop fusion | flops 35389440 | bytes 58721280 | tf_op jit(solution)/shard_map/div | solution.py:63
  99.1 10.9 %fusion.47 = (f32[128,18,512]{0,2,1:T(8,128)}, f32[128,18,512]{0,2,1:T(8,128)}) fusion(f32[128,24,512]{0,2,1:T(8,128)} %multiply_add_fusion, f32[128]{0:T(128)S(1)} %dynamic_slice.11, f32[128,20,512]{0,2,1:T(8,128)S(1)} %get-tuple-element.9, f32[128,20,512]{0,2,1:T(8,128)S(1)} %get-tuple-element.8, pred[18]{0:T(512)(128)(4,1)S(1)} %copy-done.45), kind=kLoop, calls=%fused_computation.74 | loop fusion | flops 31850496 | bytes 52954112 | tf_op jit(solution)/shard_map/div | solution.py:63
  110.0 21.7 %fusion.60 = f32[128,16,512]{0,2,1:T(8,128)} fusion(f32[128,18,512]{0,2,1:T(8,128)} %get-tuple-element.6, f32[128,18,512]{0,2,1:T(8,128)} %get-tuple-element.7, f32[128,22,512]{0,2,1:T(8,128)} %copy-done, f32[128,20,512]{0,2,1:T(8,128)} %copy-done.1, pred[16]{0:T(512)(128)(4,1)S(1)} %copy-done.44, pred[128]{0:T(512)(128)(4,1)S(1)} %copy-done.43, ...), kind=kLoop, calls=%fused_computation.95 | loop fusion | flops 26214400 | bytes 47186448 | tf_op jit(solution)/shard_map/jit(_where)/select_n | solution.py:114
  131.7 5.6 %copy.31 = f32[4,128,2048]{2,1,0:T(8,128)} copy(f32[4,128,2048]{1,2,0:T(8,128)} %bitcast.30) | data formatting | bytes 8388608 | tf_op jit(solution)/shard_map/transpose | solution.py:29
  137.3 5.8 %all-to-all-start = ((f32[2,2,128,2048]{3,2,1,0:T(8,128)}), f32[2,2,128,2048]{3,2,1,0:T(8,128)}, u32[]{:S(2)}, u32[]{:S(2)}) async-start(f32[2,2,128,2048]{3,2,1,0:T(8,128)} %bitcast.31), calls=%async_computation | async-start | bytes 8388608 | tf_op jit(solution)/shard_map/all_to_all | solution.py:42
  143.0 0.0 all-reduce.10.cloned.1.call-start
  143.1 0.1 eq.141
  143.2 0.1 compare_convert_fusion
  143.3 0.1 fusion.81
  143.4 5.1 %fusion.82 = f32[512,2048]{1,0:T(8,128)} fusion(f32[69,2048]{1,0:T(8,128)S(1)} %copy-done.5, f32[512,1]{0,1:T(1,128)S(1)} %bitcast.32, f32[512,4]{0,1:T(4,128)S(1)} %compare_convert_fusion, f32[512,64]{0,1:T(8,128)S(1)} %fusion.81), kind=kOutput, calls=%fused_computation.130 | convolution fusion | flops 868291584 | bytes 4900864 | tf_op jit(solution)/shard_map/dot_general | solution.py:119
  148.5 42.2 %all-to-all-done = f32[2,2,128,2048]{3,2,1,0:T(8,128)} async-done(((f32[2,2,128,2048]{3,2,1,0:T(8,128)}), f32[2,2,128,2048]{3,2,1,0:T(8,128)}, u32[]{:S(2)}, u32[]{:S(2)}) %all-to-all-start) | async-done | bytes 4194336 | tf_op jit(solution)/shard_map/all_to_all | solution.py:42
  190.6 2.6 copy.32
  193.2 0.0 slice-start.1
  193.3 9.2 %all_to_all.10 = f32[2,2,128,2048]{3,2,0,1:T(8,128)S(1)} all-to-all(f32[2,2,128,2048]{3,2,0,1:T(8,128)S(1)} %copy.32), channel_id=1, replica_groups=mesh['grp_0'=2,'grp_1'=2,'tile'=32] {'grp_1'}, dimensions={1} | all-to-all | bytes 8388608 | tf_op jit(solution)/shard_map/all_to_all | solution.py:42
  202.5 0.5 copy.33
  203.0 1.7 copy-done.4
  204.7 6.1 %convert_reduce_fusion = (f32[2048]{0:T(1024)S(1)}, bf16[512,2048]{1,0:T(8,128)(2,1)}, f32[512,2048]{1,0:T(8,128)S(1)}) fusion(f32[2,2,128,2048]{3,2,1,0:T(8,128)S(1)} %copy.33, f32[2048]{0:T(1024)S(1)} %copy-done.23, bf16[2048,2048]{1,0:T(8,128)(2,1)S(1)} %bitcast.35, f32[512,2048]{1,0:T(8,128)S(1)} %copy-done.4), kind=kOutput, calls=%fused_computation.121 | convolution fusion | flops 4307548160 | bytes 23085056 | tf_op jit(solution)/shard_map/dot_general | solution.py:122
  210.8 6.1 %fusion.86 = f32[512,2048]{1,0:T(8,128)} fusion(bf16[2048,2048]{1,0:T(8,128)(2,1)S(1)} %bitcast.35, f32[512,2048]{1,0:T(8,128)S(1)} %get-tuple-element.37), kind=kOutput, calls=%fused_computation.164 | convolution fusion | flops 4297064448 | bytes 16777216 | tf_op jit(solution)/shard_map/dot_general | solution.py:133
  216.8 7.0 %fusion.74 = f32[69,2048]{1,0:T(8,128)} fusion(f32[512,2048]{1,0:T(8,128)} %fusion.86, f32[512,2048]{1,0:T(8,128)S(1)} %copy-done.4, f32[512,1]{0,1:T(1,128)S(1)} %bitcast.33, f32[512,4]{0,1:T(4,128)S(1)} %compare_convert_fusion, f32[512,64]{0,1:T(8,128)S(1)} %fusion.81), kind=kOutput, calls=%fused_computation.115 | convolution fusion | flops 876680192 | bytes 9095168 | tf_op jit(solution)/shard_map/dot_general | solution.py:136
  223.8 0.0 all-reduce.10.cloned.1.call-update
  223.9 14.6 %subtract_convert_fusion = bf16[2048,2048]{1,0:T(8,128)(2,1)} fusion(bf16[2048,2048]{1,0:T(8,128)(2,1)} %param.14, f32[512,2048]{1,0:T(8,128)} %copy-done.47, f32[512,2048]{1,0:T(8,128)} %fusion.82), kind=kOutput, calls=%fused_computation | convolution fusion | flops 4319084544 | bytes 25165824 | tf_op jit(solution)/shard_map/dot_general | solution.py:127
  238.5 0.6 multiply_subtract_fusion.1
  239.1 135.0 %all-reduce.10.cloned.1.call-done = f32[69,2048]{1,0:T(8,128)} async-done(((f32[69,2048]{1,0:T(8,128)}), f32[69,2048]{1,0:T(8,128)}) %all-reduce.10.cloned.1.call-update) | async-done | bytes 565264 | tf_op jit(solution)/shard_map/psum | solution.py:139
  374.0 1.9 multiply_subtract_fusion
  (92 shorter events, 0.3 us)
Async XLA Ops:
  7.2 16.4 %copy-start.22 = (s32[512,8]{0,1:T(8,128)S(1)}, s32[512,8]{0,1:T(8,128)}, u32[]{:S(2)}) copy-start(s32[512,8]{0,1:T(8,128)} %param.10) | copy-start | bytes 49156
  8.0 25.9 %collective-permute-start.2 = (s32[4,512]{1,0:T(4,128)S(1)}, s32[4,512]{1,0:T(4,128)S(1)}, u32[]{:S(2)}, u32[]{:S(2)}) collective-permute-start(s32[4,512]{1,0:T(4,128)S(1)} %get-tuple-element.24), channel_id=1, source_target_pairs={{0,1},{1,2},{2,3},{3,4},{4,5},{5,6},{6,7},{7,8},{8,9},{9,10},{10,1... | collective-permute-start | bytes 24584 | tf_op jit(solution)/shard_map/ppermute | solution.py:20
  12.3 21.6 %collective-permute-start.3 = (s32[4,512]{1,0:T(4,128)S(1)}, s32[4,512]{1,0:T(4,128)S(1)}, u32[]{:S(2)}, u32[]{:S(2)}) collective-permute-start(s32[4,512]{1,0:T(4,128)S(1)} %get-tuple-element.25), channel_id=1, source_target_pairs={{1,0},{2,1},{3,2},{4,3},{5,4},{6,5},{7,6},{8,7},{9,8},{10,9},{11,1... | collective-permute-start | bytes 24584 | tf_op jit(solution)/shard_map/ppermute | solution.py:21
  16.7 32.2 %collective-permute-start = (f32[128,4,512]{2,0,1:T(8,128)S(1)}, f32[128,4,512]{2,0,1:T(8,128)S(1)}, u32[]{:S(2)}, u32[]{:S(2)}) collective-permute-start(f32[128,4,512]{2,0,1:T(8,128)S(1)} %copy.34), channel_id=1, source_target_pairs={{0,1},{1,2},{2,3},{3,4},{4,5},{5,6},{6,7},{7,8},{8,9},{9,10},{10,1... | collective-permute-start | bytes 3145736 | tf_op jit(solution)/shard_map/ppermute | solution.py:20
  22.3 27.0 %collective-permute-start.1 = (f32[128,4,512]{2,0,1:T(8,128)}, f32[128,4,512]{2,0,1:T(8,128)}, u32[]{:S(2)}, u32[]{:S(2)}) collective-permute-start(f32[128,4,512]{2,0,1:T(8,128)} %copy.35), channel_id=1, source_target_pairs={{1,0},{2,1},{3,2},{4,3},{5,4},{6,5},{7,6},{8,7},{9,8},{10,9},{11,1... | collective-permute-start | bytes 3145736 | tf_op jit(solution)/shard_map/ppermute | solution.py:21
  23.6 25.2 %copy-start.24 = (f32[128]{0:T(128)}, f32[128]{0:T(128)S(1)}, u32[]{:S(2)}) copy-start(f32[128]{0:T(128)S(1)} %get-tuple-element.27) | copy-start | bytes 1540
  23.6 25.2 %copy-start.26 = (f32[128]{0:T(128)}, f32[128]{0:T(128)S(1)}, u32[]{:S(2)}) copy-start(f32[128]{0:T(128)S(1)} %get-tuple-element.28) | copy-start | bytes 1540
  23.6 25.2 %copy-start.28 = (f32[128]{0:T(128)}, f32[128]{0:T(128)S(1)}, u32[]{:S(2)}) copy-start(f32[128]{0:T(128)S(1)} %get-tuple-element.29) | copy-start | bytes 1540
  23.6 25.2 %copy-start.30 = (f32[128]{0:T(128)}, f32[128]{0:T(128)S(1)}, u32[]{:S(2)}) copy-start(f32[128]{0:T(128)S(1)} %get-tuple-element.30) | copy-start | bytes 1540
  23.6 25.2 %copy-start.32 = (f32[128]{0:T(128)}, f32[128]{0:T(128)S(1)}, u32[]{:S(2)}) copy-start(f32[128]{0:T(128)S(1)} %get-tuple-element.31) | copy-start | bytes 1540
  23.7 25.2 %copy-start.34 = (f32[128]{0:T(128)}, f32[128]{0:T(128)S(1)}, u32[]{:S(2)}) copy-start(f32[128]{0:T(128)S(1)} %get-tuple-element.32) | copy-start | bytes 1540
  23.7 25.2 %copy-start.36 = (f32[128]{0:T(128)}, f32[128]{0:T(128)S(1)}, u32[]{:S(2)}) copy-start(f32[128]{0:T(128)S(1)} %get-tuple-element.33) | copy-start | bytes 1540
  33.9 15.0 %copy-start.6 = (f32[24,512]{1,0:T(8,128)}, f32[24,512]{1,0:T(8,128)S(1)}, u32[]{:S(2)}) copy-start(f32[24,512]{1,0:T(8,128)S(1)} %get-tuple-element.22) | copy-start | bytes 147460
  33.9 15.0 %copy-start.8 = (f32[24,512]{1,0:T(8,128)}, f32[24,512]{1,0:T(8,128)S(1)}, u32[]{:S(2)}) copy-start(f32[24,512]{1,0:T(8,128)S(1)} %get-tuple-element.23) | copy-start | bytes 147460
  34.0 14.9 %copy-start.10 = (f32[24,512]{1,0:T(8,128)}, f32[24,512]{1,0:T(8,128)S(1)}, u32[]{:S(2)}) copy-start(f32[24,512]{1,0:T(8,128)S(1)} %get-tuple-element.16) | copy-start | bytes 147460
  34.0 14.9 %copy-start.12 = (f32[24,512]{1,0:T(8,128)}, f32[24,512]{1,0:T(8,128)S(1)}, u32[]{:S(2)}) copy-start(f32[24,512]{1,0:T(8,128)S(1)} %get-tuple-element.17) | copy-start | bytes 147460
  34.0 14.9 %copy-start.14 = (f32[24,512]{1,0:T(8,128)}, f32[24,512]{1,0:T(8,128)S(1)}, u32[]{:S(2)}) copy-start(f32[24,512]{1,0:T(8,128)S(1)} %get-tuple-element.18) | copy-start | bytes 147460
  34.0 14.9 %copy-start.16 = (f32[24,512]{1,0:T(8,128)}, f32[24,512]{1,0:T(8,128)S(1)}, u32[]{:S(2)}) copy-start(f32[24,512]{1,0:T(8,128)S(1)} %get-tuple-element.19) | copy-start | bytes 147460
  34.0 14.9 %copy-start.18 = (f32[24,512]{1,0:T(8,128)}, f32[24,512]{1,0:T(8,128)S(1)}, u32[]{:S(2)}) copy-start(f32[24,512]{1,0:T(8,128)S(1)} %get-tuple-element.20) | copy-start | bytes 147460
  34.0 14.9 %copy-start.20 = (f32[24,512]{1,0:T(8,128)}, f32[24,512]{1,0:T(8,128)S(1)}, u32[]{:S(2)}) copy-start(f32[24,512]{1,0:T(8,128)S(1)} %get-tuple-element.21) | copy-start | bytes 147460
  50.9 1.0 copy-start.3
  51.9 3.4 copy-start.2
  51.9 3.4 copy-start.7
  51.9 3.5 copy-start.9
  51.9 3.5 copy-start.11
  51.9 3.4 copy-start.13
  51.9 3.4 copy-start.15
  51.9 3.4 copy-start.17
  51.9 3.4 copy-start.19
  51.9 3.4 copy-start.21
  51.9 3.4 copy-start.25
  51.9 3.4 copy-start.27
  51.9 3.4 copy-start.29
  51.9 3.4 copy-start.31
  52.0 3.4 copy-start.33
  52.0 3.4 copy-start.35
  52.0 3.4 copy-start.37
  71.1 11.3 %copy-start.46 = (pred[20]{0:T(512)(128)(4,1)S(1)}, pred[20]{0:T(512)(128)(4,1)}, u32[]{:S(2)}) copy-start(pred[20]{0:T(512)(128)(4,1)} %compare_and_fusion.1) | copy-start | bytes 64
  82.4 16.6 %copy-start = (f32[128,22,512]{0,2,1:T(8,128)}, f32[128,22,512]{0,2,1:T(8,128)S(1)}, u32[]{:S(2)}) copy-start(f32[128,22,512]{0,2,1:T(8,128)S(1)} %get-tuple-element.11) | copy-start | bytes 17301508
  82.4 16.7 %copy-start.45 = (pred[18]{0:T(512)(128)(4,1)S(1)}, pred[18]{0:T(512)(128)(4,1)}, u32[]{:S(2)}) copy-start(pred[18]{0:T(512)(128)(4,1)} %compare_and_fusion.2) | copy-start | bytes 58
  99.0 10.9 %copy-start.1 = (f32[128,20,512]{0,2,1:T(8,128)}, f32[128,20,512]{0,2,1:T(8,128)S(1)}, u32[]{:S(2)}) copy-start(f32[128,20,512]{0,2,1:T(8,128)S(1)} %get-tuple-element.9) | copy-start | bytes 15728644
  99.0 10.9 %copy-start.40 = (pred[128]{0:T(512)(128)(4,1)S(1)}, pred[128]{0:T(512)(128)(4,1)}, u32[]{:S(2)}) copy-start(pred[128]{0:T(512)(128)(4,1)} %get-tuple-element.4) | copy-start | bytes 388
  99.0 10.9 %copy-start.41 = (pred[128]{0:T(512)(128)(4,1)S(1)}, pred[128]{0:T(512)(128)(4,1)}, u32[]{:S(2)}) copy-start(pred[128]{0:T(512)(128)(4,1)} %get-tuple-element.34) | copy-start | bytes 388
  99.0 10.9 %copy-start.42 = (pred[128]{0:T(512)(128)(4,1)S(1)}, pred[128]{0:T(512)(128)(4,1)}, u32[]{:S(2)}) copy-start(pred[128]{0:T(512)(128)(4,1)} %get-tuple-element.35) | copy-start | bytes 388
  99.1 10.9 %copy-start.43 = (pred[128]{0:T(512)(128)(4,1)S(1)}, pred[128]{0:T(512)(128)(4,1)}, u32[]{:S(2)}) copy-start(pred[128]{0:T(512)(128)(4,1)} %get-tuple-element.36) | copy-start | bytes 388
  99.1 10.9 %copy-start.44 = (pred[16]{0:T(512)(128)(4,1)S(1)}, pred[16]{0:T(512)(128)(4,1)}, u32[]{:S(2)}) copy-start(pred[16]{0:T(512)(128)(4,1)} %compare_and_fusion.3) | copy-start | bytes 52
  137.3 5.9 %copy-start.38 = (s32[512]{0:T(512)S(1)}, s32[512]{0:T(512)}, u32[]{:S(2)}) copy-start(s32[512]{0:T(512)} %param.12) | copy-start | bytes 6148
  137.3 6.1 %copy-start.5 = (f32[69,2048]{1,0:T(8,128)S(1)}, f32[69,2048]{1,0:T(8,128)}, u32[]{:S(2)}) copy-start(f32[69,2048]{1,0:T(8,128)} %param.13) | copy-start | bytes 1695748
  137.3 6.1 %copy-start.39 = (f32[512]{0:T(512)S(1)}, f32[512]{0:T(512)}, u32[]{:S(2)}) copy-start(f32[512]{0:T(512)} %param.11) | copy-start | bytes 6148
  137.3 53.4 %all-to-all-start = ((f32[2,2,128,2048]{3,2,1,0:T(8,128)}), f32[2,2,128,2048]{3,2,1,0:T(8,128)}, u32[]{:S(2)}, u32[]{:S(2)}) async-start(f32[2,2,128,2048]{3,2,1,0:T(8,128)} %bitcast.31), calls=%async_computation | async-start | bytes 8388608 | tf_op jit(solution)/shard_map/all_to_all | solution.py:42
  143.0 231.0 %all-reduce.10.cloned.1.call-start = ((), (), s32[]{:S(2)}) async-start(), calls=%async_computation.2 | async-start | bytes 1179648 | tf_op jit(solution)/shard_map/psum | solution.py:139
  190.6 12.4 %slice-start = ((s8[8388608]{0:T(1024)(128)(4,1)}), s8[4194304]{0:T(1024)(128)(4,1)S(1)}, s32[]{:S(2)}) async-start(s8[8388608]{0:T(1024)(128)(4,1)} %bitcast.34), calls=%async_computation.3 | async-start | bytes 8388608
  193.2 9.8 %slice-start.1 = ((s8[8388608]{0:T(1024)(128)(4,1)}), s8[4194304]{0:T(1024)(128)(4,1)S(1)}, s32[]{:S(2)}) async-start(s8[8388608]{0:T(1024)(128)(4,1)} %bitcast.34), calls=%async_computation.4 | async-start | bytes 8388608
  202.5 2.2 copy-start.4
  202.5 2.2 copy-start.23
  210.8 6.1 %copy-start.47 = (f32[512,2048]{1,0:T(8,128)}, f32[512,2048]{1,0:T(8,128)S(1)}, u32[]{:S(2)}) copy-start(f32[512,2048]{1,0:T(8,128)S(1)} %get-tuple-element.37) | copy-start | bytes 12582916
Sparse Core Ops, SparseCore 0:
  224.0 150.0 all-reduce.9

commit v2 on v1

v2 whole, which is shorter than its diff:
```python
import functools

import jax
import jax.numpy as jnp
from jax import lax
from jax.experimental import pallas as pl
from jax.experimental.pallas import tpu as pltpu
from jax.sharding import Mesh
from jax.sharding import PartitionSpec as P

STEPS = 4
LEVELS = 8
CLASSES = 8
AXES = ("xh", "core", "xl", "y", "z")
GRP = ("xh", "core")
TILE = ("xl", "y", "z")
BY_ID = pl.DeviceIdType.MESH
MIB = 2**20
CHUNKS = 8
SUB = 8


def place():
    return {axis: lax.axis_index(axis) for axis in AXES}


def at(here, **moved):
    return tuple(moved.get(axis, here[axis]) for axis in AXES)


def beside(here, step):
    tile = here["xl"] * 16 + here["y"] * 4 + here["z"] + step
    tile = (tile + 32) % 32
    return at(here, xl=tile // 16, y=(tile // 4) % 4, z=tile % 4)


def solve_kernel(
    field_ref, class_ref, table_ref, steep_ref, pick_ref, target_ref,
    raw, rows_own, halo_up, halo_dn, class_up, class_dn, kappa, wide_a, wide_b, sent, got,
    load_sem, halo_send, halo_recv, class_send, class_recv, out_send, out_recv, keep_sem,
):
    here = place()
    runs = rows_own.shape[1]
    tile_rows = rows_own.shape[0]
    width = rows_own.shape[2]
    part = runs // CHUNKS
    tile = here["xl"] * 16 + here["y"] * 4 + here["z"]
    group = here["xh"] * 2 + here["core"]
    up, dn = beside(here, -1), beside(here, 1)
    has_up, has_dn = tile > 0, tile < 31
    mates = (
        (here["xh"] * 2 + 1 - here["core"], at(here, core=1 - here["core"])),
        ((1 - here["xh"]) * 2 + here["core"], at(here, xh=1 - here["xh"])),
        ((1 - here["xh"]) * 2 + 1 - here["core"], at(here, xh=1 - here["xh"], core=1 - here["core"])),
    )

    def load(k):
        lines = part * tile_rows
        return [
            pltpu.make_async_copy(
                field_ref.at[pl.ds(k * lines, lines), pl.ds(128 * c, 128)],
                raw.at[c, pl.ds(k * lines, lines)],
                load_sem.at[k, c],
            )
            for c in range(width // 128)
        ]

    for k in range(CHUNKS):
        for copy in load(k):
            copy.start()

    barrier = pltpu.get_barrier_semaphore()
    for _, mate in mates:
        pl.semaphore_signal(barrier, inc=1, device_id=mate, device_id_type=BY_ID)

    @pl.when(has_up)
    def _():
        pl.semaphore_signal(barrier, inc=1, device_id=up, device_id_type=BY_ID)

    @pl.when(has_dn)
    def _():
        pl.semaphore_signal(barrier, inc=1, device_id=dn, device_id_type=BY_ID)

    callers = 3 + jnp.where(has_up, 1, 0) + jnp.where(has_dn, 1, 0)
    pl.semaphore_wait(barrier, callers)

    def class_copy(upward):
        return pltpu.make_async_remote_copy(
            src_ref=class_ref.at[pl.ds(0 if upward else tile_rows - STEPS, STEPS)],
            dst_ref=class_dn if upward else class_up,
            send_sem=class_send.at[0 if upward else 1],
            recv_sem=class_recv.at[0 if upward else 1],
            device_id=up if upward else dn,
            device_id_type=BY_ID,
        )

    def halo_copy(k, upward):
        span = pl.ds(pl.multiple_of(k * part, part), part)
        return pltpu.make_async_remote_copy(
            src_ref=rows_own.at[pl.ds(0 if upward else tile_rows - STEPS, STEPS), span],
            dst_ref=(halo_dn if upward else halo_up).at[:, span],
            send_sem=halo_send.at[k, 0 if upward else 1],
            recv_sem=halo_recv.at[k, 0 if upward else 1],
            device_id=up if upward else dn,
            device_id_type=BY_ID,
        )

    def out_copy(k, j):
        span = pl.ds(pl.multiple_of(k * part, part), part)
        owner, mate = mates[j]
        return pltpu.make_async_remote_copy(
            src_ref=sent.at[owner, span],
            dst_ref=got.at[j, span],
            send_sem=out_send.at[k, j],
            recv_sem=out_recv.at[k, j],
            device_id=mate,
            device_id_type=BY_ID,
        )

    @pl.when(has_up)
    def _():
        class_copy(True).start()

    @pl.when(has_dn)
    def _():
        class_copy(False).start()

    @pl.when(jnp.logical_not(has_up))
    def _():
        halo_up[...] = jnp.zeros_like(halo_up)
        class_up[...] = jnp.full_like(class_up, -1)

    @pl.when(jnp.logical_not(has_dn))
    def _():
        halo_dn[...] = jnp.zeros_like(halo_dn)
        class_dn[...] = jnp.full_like(class_dn, -1)

    for k in range(CHUNKS):
        for copy in load(k):
            copy.wait()

        def turn(j, carry):
            first = pl.multiple_of(j * SUB, SUB)
            for i in range(tile_rows):
                for c in range(width // 128):
                    rows_own[i, pl.ds(first, SUB), pl.ds(128 * c, 128)] = raw[
                        c, pl.ds(j * (SUB * tile_rows) + i, SUB, stride=tile_rows), :
                    ]
            return carry

        lax.fori_loop(k * part // SUB, (k + 1) * part // SUB, turn, 0)

        @pl.when(has_up)
        def _():
            halo_copy(k, True).start()

        @pl.when(has_dn)
        def _():
            halo_copy(k, False).start()

    @pl.when(has_up)
    def _():
        class_copy(False).wait_recv()

    @pl.when(has_dn)
    def _():
        class_copy(True).wait_recv()

    keep_up = jnp.where(has_up, 1.0, 0.0).astype(jnp.float32)
    keep_dn = jnp.where(has_dn, 1.0, 0.0).astype(jnp.float32)
    lane = lax.broadcasted_iota(jnp.int32, (SUB, width), 1)
    left, right = lane == 0, lane == width - 1
    span_rows = tile_rows + 2 * STEPS

    def advance(s, carry):
        first = pl.multiple_of(s * SUB, SUB)
        runs_here = pl.ds(first, SUB)
        steep = jnp.broadcast_to(steep_ref[runs_here, 0:1], (SUB, width))
        rest = 1.0 - steep
        pick = jnp.broadcast_to(pick_ref[runs_here, 0:1], (SUB, width))
        half = [
            jnp.broadcast_to(table_ref[runs_here, c : c + 1], (SUB, width)) for c in range(CLASSES)
        ]
        for i in range(span_rows):
            if i < STEPS:
                klass = class_up[i]
            elif i < STEPS + tile_rows:
                klass = class_ref[i - STEPS]
            else:
                klass = class_dn[i - STEPS - tile_rows]
            value = jnp.zeros((SUB, width), jnp.float32)
            for c in range(CLASSES):
                value = jnp.where(klass == c, half[c], value)
            kappa[i] = value

        def start_row(i):
            if i < STEPS:
                return halo_up[i, runs_here]
            if i < STEPS + tile_rows:
                return rows_own[i - STEPS, runs_here]
            return halo_dn[i - STEPS - tile_rows, runs_here]

        for step in range(STEPS):
            source = (None, wide_a, wide_b, wide_a)[step]
            sink = (wide_a, wide_b, wide_a, None)[step]

            def row(i):
                return start_row(i) if step == 0 else source[i]

            def spread_of(i, value):
                bottom = 1.0 + value * value
                guess = pl.reciprocal(bottom, approx=True)
                guess = guess * (2.0 - bottom * guess)
                return kappa[i] * (steep + rest * guess)

            above = row(step)
            above_spread = spread_of(step, above)
            centre = row(step + 1)
            spread = spread_of(step + 1, centre)
            flow_in = (above_spread + spread) * (centre - above)
            for i in range(step + 1, span_rows - step - 1):
                below = row(i + 1)
                below_spread = spread_of(i + 1, below)
                flow_out = (spread + below_spread) * (below - centre)
                beyond = jnp.where(right, 0.0, pltpu.roll(centre, width - 1, 1))
                beyond_spread = jnp.where(right, 0.0, pltpu.roll(spread, width - 1, 1))
                flow = (spread + beyond_spread) * (beyond - centre)
                back = jnp.where(left, spread * centre, pltpu.roll(flow, 1, 1))
                total = centre + (flow_out - flow_in) + (flow - back)
                if i < STEPS:
                    total = total * keep_up
                if i >= STEPS + tile_rows:
                    total = total * keep_dn
                if sink is not None:
                    sink[i] = total
                if STEPS <= i < STEPS + tile_rows:
                    owner, inner = (i - STEPS) // 4, (i - STEPS) % 4
                    columns = pl.ds(inner * width, width)
                    if step > 0:
                        total = jnp.where(pick == step + 1, total, sent[owner, runs_here, columns])
                    sent[owner, runs_here, columns] = total
                flow_in, centre, spread = flow_out, below, below_spread
        return carry

    for k in range(CHUNKS):
        @pl.when(has_up)
        def _():
            halo_copy(k, False).wait_recv()

        @pl.when(has_dn)
        def _():
            halo_copy(k, True).wait_recv()

        lax.fori_loop(k * part // SUB, (k + 1) * part // SUB, advance, 0)
        for j in range(3):
            out_copy(k, j).start()

    def keep(j):
        if j == 3:
            source, owner = sent.at[group], group
        else:
            source, owner = got.at[j], mates[j][0]
        return pltpu.make_async_copy(
            source, target_ref.at[pl.ds(pl.multiple_of(owner * runs, runs), runs)], keep_sem.at[j]
        )

    keep(3).start()
    for j in range(3):
        for k in range(CHUNKS):
            out_copy(k, j).wait_recv()
        keep(j).start()
    for j in range(4):
        keep(j).wait()
    for k in range(CHUNKS):
        for j in range(3):
            out_copy(k, j).wait_send()

    @pl.when(has_up)
    def _():
        class_copy(True).wait_send()
        for k in range(CHUNKS):
            halo_copy(k, True).wait_send()

    @pl.when(has_dn)
    def _():
        class_copy(False).wait_send()
        for k in range(CHUNKS):
            halo_copy(k, False).wait_send()


def solve(field, classes, table, steep, pick):
    runs, rows, width = field.shape
    f32 = jnp.float32
    dma = pltpu.SemaphoreType.DMA
    vmem = pl.BlockSpec(memory_space=pltpu.VMEM)
    anywhere = pl.BlockSpec(memory_space=pl.ANY)
    wide = jnp.broadcast_to(classes[:, None, :], (rows, SUB, width))
    return pl.pallas_call(
        solve_kernel,
        out_shape=jax.ShapeDtypeStruct((4 * runs, 4 * width), f32),
        in_specs=[anywhere, vmem, vmem, vmem, vmem],
        out_specs=anywhere,
        scratch_shapes=[
            pltpu.VMEM((width // 128, runs * rows, 128), f32),
            pltpu.VMEM((rows, runs, width), f32),
            pltpu.VMEM((STEPS, runs, width), f32),
            pltpu.VMEM((STEPS, runs, width), f32),
            pltpu.VMEM((STEPS, SUB, width), jnp.int32),
            pltpu.VMEM((STEPS, SUB, width), jnp.int32),
            pltpu.VMEM((rows + 2 * STEPS, SUB, width), f32),
            pltpu.VMEM((rows + 2 * STEPS, SUB, width), f32),
            pltpu.VMEM((rows + 2 * STEPS, SUB, width), f32),
            pltpu.VMEM((4, runs, 4 * width), f32),
            pltpu.VMEM((3, runs, 4 * width), f32),
            dma((CHUNKS, 4)),
            dma((CHUNKS, 2)),
            dma((CHUNKS, 2)),
            dma((2,)),
            dma((2,)),
            dma((CHUNKS, 3)),
            dma((CHUNKS, 3)),
            dma((4,)),
        ],
        compiler_params=pltpu.CompilerParams(
            collective_id=1, has_side_effects=True, vmem_limit_bytes=48 * MIB
        ),
        name="solve",
    )(field.reshape(runs * rows, width), wide, table, steep, pick)


def sum_kernel(
    part_ref, out_ref, pair, own, landed, mine,
    pair_send, pair_recv, part_send, part_recv, back_send, back_recv, last_send, last_recv,
):
    here = place()
    core = here["core"]
    chips = own.shape[0]
    chip = here["xh"] * 32 + here["xl"] * 16 + here["y"] * 4 + here["z"]
    mate = at(here, core=1 - core)

    def device(k):
        return (k // 32, core, (k // 16) % 2, (k // 4) % 4, k % 4)

    barrier = pltpu.get_barrier_semaphore()
    pl.semaphore_signal(barrier, inc=1, device_id=mate, device_id_type=BY_ID)

    def greet(j, carry):
        pl.semaphore_signal(
            barrier, inc=1, device_id=device((chip + j) % chips), device_id_type=BY_ID
        )
        return carry

    lax.fori_loop(1, chips, greet, 0)
    pl.semaphore_wait(barrier, chips)

    swap = pltpu.make_async_remote_copy(
        src_ref=part_ref.at[pl.ds((1 - core) * chips, chips)],
        dst_ref=pair,
        send_sem=pair_send,
        recv_sem=pair_recv,
        device_id=mate,
        device_id_type=BY_ID,
    )
    swap.start()
    swap.wait_recv()
    own[...] = part_ref[pl.ds(core * chips, chips)] + pair[...]

    def scatter(j, carry):
        other = (chip + j) % chips
        pltpu.make_async_remote_copy(
            src_ref=own.at[other],
            dst_ref=landed.at[j - 1],
            send_sem=part_send,
            recv_sem=part_recv,
            device_id=device(other),
            device_id_type=BY_ID,
        ).start()
        return carry

    lax.fori_loop(1, chips, scatter, 0)
    total = own[chip]
    whole = pltpu.make_async_remote_copy(
        src_ref=own.at[pl.ds(0, chips - 1)],
        dst_ref=landed,
        send_sem=part_send,
        recv_sem=part_recv,
        device_id=mate,
        device_id_type=BY_ID,
    )
    whole.wait_recv()
    mine[...] = total + jnp.sum(landed[...], axis=0)

    slot = core * chips + chip
    out_ref[slot] = mine[...]

    def spread(j, carry):
        pltpu.make_async_remote_copy(
            src_ref=mine,
            dst_ref=out_ref.at[slot],
            send_sem=back_send,
            recv_sem=back_recv,
            device_id=device((chip + j) % chips),
            device_id_type=BY_ID,
        ).start()
        return carry

    lax.fori_loop(1, chips, spread, 0)
    gathered = pltpu.make_async_remote_copy(
        src_ref=own.at[pl.ds(0, chips - 1)],
        dst_ref=landed,
        send_sem=back_send,
        recv_sem=back_recv,
        device_id=mate,
        device_id_type=BY_ID,
    )
    gathered.wait_recv()
    half = pl.ds(core * chips, chips)
    last = pltpu.make_async_remote_copy(
        src_ref=out_ref.at[half],
        dst_ref=out_ref.at[half],
        send_sem=last_send,
        recv_sem=last_recv,
        device_id=mate,
        device_id_type=BY_ID,
    )
    last.start()
    last.wait()
    swap.wait_send()
    whole.wait_send()
    gathered.wait_send()


def sum_everywhere(part):
    tiles = part.shape[0]
    f32 = jnp.float32
    dma = pltpu.SemaphoreType.DMA
    vmem = pl.BlockSpec(memory_space=pltpu.VMEM)
    tile = part.shape[1:]
    return pl.pallas_call(
        sum_kernel,
        out_shape=jax.ShapeDtypeStruct(part.shape, f32),
        in_specs=[vmem],
        out_specs=vmem,
        scratch_shapes=[
            pltpu.VMEM((tiles // 2,) + tile, f32),
            pltpu.VMEM((tiles // 2,) + tile, f32),
            pltpu.VMEM((tiles // 2 - 1,) + tile, f32),
            pltpu.VMEM(tile, f32),
        ] + [dma] * 8,
        compiler_params=pltpu.CompilerParams(
            collective_id=2, has_side_effects=True, vmem_limit_bytes=16 * MIB
        ),
        name="sum_everywhere",
    )(part)


def features(run_levels, step_pick, steepness):
    count = run_levels.shape[0]
    onehot = (run_levels[:, :, None] == jnp.arange(LEVELS, dtype=jnp.int32)[None, None, :]).astype(
        jnp.float32
    )
    onehot = onehot.reshape(count, -1)
    moment = (step_pick[:, None] == jnp.arange(1, STEPS + 1, dtype=jnp.int32)[None, :]).astype(
        jnp.float32
    )
    return jnp.concatenate([onehot, moment, steepness[:, None]], axis=1)


def independent(run_levels, step_pick, steepness):
    count = run_levels.shape[0]
    f32 = jnp.float32
    onehot = (run_levels[:, :, None] == jnp.arange(LEVELS - 1, dtype=jnp.int32)).astype(f32)
    moment = (step_pick[:, None] == jnp.arange(1, STEPS, dtype=jnp.int32)).astype(f32)
    return jnp.concatenate(
        [
            onehot.reshape(count, -1),
            moment,
            steepness[:, None],
            jnp.ones((count, 1), f32),
            jnp.zeros((count, 3), f32),
        ],
        axis=1,
    )


def all_features(sums):
    width = sums.shape[1]
    classes = sums[: CLASSES * (LEVELS - 1)].reshape(CLASSES, LEVELS - 1, width)
    first = CLASSES * (LEVELS - 1)
    moment = sums[first : first + STEPS - 1]
    steep = sums[first + STEPS - 1 : first + STEPS]
    ones = sums[first + STEPS : first + STEPS + 1]
    last = ones[None] - jnp.sum(classes, axis=1, keepdims=True)
    classes = jnp.concatenate([classes, last], axis=1).reshape(CLASSES * LEVELS, width)
    final = ones - jnp.sum(moment, axis=0, keepdims=True)
    return jnp.concatenate([classes, moment, final, steep], axis=0)


def dsilu(pre):
    logistic = jax.nn.sigmoid(pre)
    return logistic * (1.0 + pre * (1.0 - logistic))


def on_device(
    start_field, class_ids, run_levels, steepness, step_pick, input_layer, output_layer, output_bias
):
    local_runs = start_field.shape[0]
    first_run = lax.axis_index(GRP) * local_runs
    levels_here = lax.dynamic_slice_in_dim(run_levels, first_run, local_runs, 0)
    steep = lax.dynamic_slice_in_dim(steepness, first_run, local_runs, 0)[:, None]
    pick_here = lax.dynamic_slice_in_dim(step_pick, first_run, local_runs, 0)[:, None]
    table = 0.015 * jnp.exp(levels_here.astype(jnp.float32) * jnp.log(jnp.float32(1.35)))
    target = solve(start_field, class_ids, table, steep, pick_here)
    runs_total = target.shape[0]
    feats = features(run_levels, step_pick, steepness)
    pre = jnp.dot(feats, input_layer, precision=lax.Precision.HIGHEST)
    hidden = jax.nn.silu(pre).astype(jnp.bfloat16)
    error = (
        jnp.dot(hidden, output_layer, preferred_element_type=jnp.float32)
        + output_bias[None, :]
        - target
    )
    slope = (error * (2.0 / runs_total)).astype(jnp.bfloat16)
    grad = lax.dot_general(
        hidden, slope, (((0,), (0,)), ((), ())), preferred_element_type=jnp.float32
    )
    output_next = (output_layer.astype(jnp.float32) - 0.5 * grad).astype(jnp.bfloat16)
    bias_next = output_bias - 0.5 * jnp.sum(slope.astype(jnp.float32), axis=0)
    gain_slope = dsilu(pre)
    partial_back = lax.dot_general(
        slope, output_layer, (((1,), (1,)), ((), ())), preferred_element_type=jnp.float32
    )
    basis = independent(run_levels, step_pick, steepness)
    partial_in = lax.dot_general(
        basis, partial_back * gain_slope, (((0,), (0,)), ((), ())), precision=lax.Precision.HIGHEST
    )
    width = partial_in.shape[1]
    tiles = partial_in.reshape(8, 8, width // 128, 128).transpose(0, 2, 1, 3).reshape(-1, 8, 128)
    tiles = sum_everywhere(tiles)
    sums = tiles.reshape(8, width // 128, 8, 128).transpose(0, 2, 1, 3).reshape(64, width)
    input_next = input_layer - 2.0 * all_features(sums)
    return (error.astype(jnp.bfloat16), output_next, bias_next, input_next)


def solution(mesh):
    split = Mesh(mesh.devices.reshape(2, 2, 2, 4, 4), AXES)
    return jax.shard_map(
        on_device,
        mesh=split,
        in_specs=(
            P(GRP, TILE, None),
            P(TILE, None),
            P(),
            P(),
            P(),
            P(),
            P(None, GRP + TILE),
            P(GRP + TILE),
        ),
        out_specs=(P(None, GRP + TILE), P(None, GRP + TILE), P(GRP + TILE), P()),
        check_vma=False,
    )
```

time: 384 us -> 176 us (0.46)
  waiting for transfers between devices: 177 us -> 0 us
  Pallas kernels: 0 us -> 129 us
  other arithmetic: 101 us -> 5 us
  local copies, waits for them, and re-layouts: 24.5 us -> 4.63 us
  starting transfers between devices: 17 us -> 0 us
  between operations: 14.8 us -> 0.84 us
  blocking collectives: 9.24 us -> 0 us
    psum x1 -> x0, waiting for transfers between devices: 135 us -> none  [on_device(): grad_in = lax.psum(partial_in, GRP_TILE)]
    pallas_call x0 -> x2, Pallas kernels: none -> 129 us  [the longest x1 102 us: solve(): pl.pallas_call(solve_kernel, out_shape=jax.ShapeDtypeStruct((4 * runs, 4...]
    div x4 -> x0, other arithmetic: 54.4 us -> none  [advance(): spread = kappa * (1.0 + steep * ratio) / (1.0 + ratio)]
    all_to_all x1 -> x0, waiting for transfers between devices: 42.2 us -> none  [turned_blocks(): out = lax.all_to_all(out, axes[k], k, k, tiled=True)]
    select_n x3 -> x0, other arithmetic: 21.8 us -> none  [the longest x1 21.7 us: on_device(): jnp.where(pick_here == step + 1, wide[:, margin:margin + rows], snapshot)]
    add x2 -> x1, other arithmetic: 15.6 us -> 0.01 us  [independent(): jnp.arange(1, STEPS, dtype=jnp.int32)]
    ppermute x4 -> x0, starting transfers between devices: 11.2 us -> none  [the longest x2 8.61 us: with_halo(): before = lax.ppermute(last, axis, up)]
    unnamed x103 -> x9, local copies, waits for them, and re-layouts: 10.4 us -> 0.19 us
  transfers between devices with their start and end apart: 6 -> 0, of which waited for: 2 -> 0; matrix products, arithmetic and copies ran while one was open for 13% -> 0% of each run, Pallas kernels for 0% -> 0%
where the time goes in v2:
time: 176 us
  Pallas kernels  129 us (73%)
  matrix products  35.9 us (20%)
  other arithmetic  5 us (3%)
  local copies, waits for them, and re-layouts  4.63 us (3%)
    pallas_call x1, Pallas kernels, solve(): pl.pallas_call(solve_kernel, out_shape=jax.ShapeDtypeStruct((4 * runs, 4...  102 us
    pallas_call x1, Pallas kernels, sum_everywhere(): pl.pallas_call(sum_kernel, out_shape=jax.ShapeDtypeStruct(part.shape, f32...  27.8 us
    dot_general x1, matrix products, on_device(): lax.dot_general(hidden, slope, (((0,), (0,)), ((), ())), preferred_elemen...  10.9 us
    dot_general x1, matrix products, on_device(): jnp.dot(hidden, output_layer, preferred_element_type=jnp.float32)  9.38 us
    dot_general x1, matrix products, on_device(): lax.dot_general(slope, output_layer, (((1,), (1,)), ((), ())), preferred_...  8.08 us
    dot_general x1, matrix products, on_device(): lax.dot_general(basis, partial_back * gain_slope, (((0,), (0,)), ((), ())...  4 us
    dot_general x1, matrix products, on_device(): pre = jnp.dot(feats, input_layer, precision=lax.Precision.HIGHEST)  3.55 us

profile of v2, /device:TPU:1, one launch (start us, length us, event | category | flops | bytes accessed | tf_op | source)
XLA Modules:
  0.0 175.7 jit_solution(8037009751073595684)
XLA Ops:
  0.6 0.8 dynamic-slice_bitcast_fusion.1
  1.4 0.8 dynamic-slice_bitcast_fusion
  2.2 0.7 multiply_exponential_fusion
  2.9 0.1 eq.78
  2.9 0.1 eq.69
  3.0 0.8 compare_convert_fusion.1
  3.8 0.8 compare_convert_fusion.2
  4.5 0.1 copy.22
  4.6 0.1 copy.24.pick_ref
  4.8 0.1 copy.23.steep_ref
  4.9 0.8 fusion.14
  5.7 0.7 eq.75
  6.4 0.1 compare_convert_fusion
  6.5 0.7 concatenate.13
  7.2 0.8 broadcast_in_dim.15.class_ref
  8.0 0.0 copy-start
  8.0 0.0 copy-start.1
  8.0 101.5 %solve.1 = f32[512,2048]{1,0:T(8,128)S(1)} custom-call(f32[2048,512]{1,0:T(8,128)} %bitcast.40, s32[16,8,512]{2,1,0:T(8,128)S(1)} %broadcast_in_dim.15.class_ref, f32[128,8]{1,0:T(8,128)S(1)} %broadcast_multiply_fusion.table_ref, f32[128,1]{1,0:T(8,128)S(1)} %copy.23.steep_ref, s32[128,1]{1,0:T(8,128)S(1)} %copy.24.pick_ref), custom_call_target="tpu_custom_call" | custom-call | tf_op jit(solution)/shard_map/solve/pallas_call | solution.py:298
  109.6 0.0 copy-done
  109.6 0.0 copy-done.1
  109.6 0.0 copy-start.2
  109.6 3.6 %fusion.8 = f32[512,2048]{1,0:T(8,128)S(1)} fusion(f32[69,2048]{1,0:T(8,128)S(1)} %copy-done, f32[512,1]{0,1:T(1,128)S(1)} %bitcast.46, f32[512,4]{0,1:T(4,128)S(1)} %compare_convert_fusion.2, f32[512,64]{0,1:T(8,128)S(1)} %fusion.14), kind=kOutput, calls=%fused_computation.18 | convolution fusion | flops 868291584 | bytes 4900864 | tf_op jit(solution)/shard_map/dot_general | solution.py:516
  113.1 0.0 copy-done.2
  113.2 9.4 %convert_reduce_fusion = (f32[2048]{0:T(1024)S(1)}, bf16[512,2048]{1,0:T(8,128)(2,1)}, f32[512,2048]{1,0:T(8,128)S(1)}) fusion(f32[512,2048]{1,0:T(8,128)S(1)} %solve.1, f32[2048]{0:T(1024)S(1)} %copy-done.2, bf16[2048,2048]{1,0:T(8,128)(2,1)} %param.14, f32[512,2048]{1,0:T(8,128)S(1)} %fusion.8), kind=kOutput, calls=%fused_computation.7 | convolution fusion | flops 4307548160 | bytes 23085056 | tf_op jit(solution)/shard_map/dot_general | solution.py:519
  122.5 0.0 copy-start.3
  122.5 0.6 multiply_subtract_fusion
  123.2 8.1 %fusion.17 = f32[512,2048]{1,0:T(8,128)S(1)} fusion(bf16[2048,2048]{1,0:T(8,128)(2,1)} %param.14, f32[512,2048]{1,0:T(8,128)S(1)} %get-tuple-element.11), kind=kOutput, calls=%fused_computation.41 | convolution fusion | flops 4297064448 | bytes 16777216 | tf_op jit(solution)/shard_map/dot_general | solution.py:530
  131.3 0.0 copy-done.3
  131.3 4.0 %fusion = f32[64,2048]{1,0:T(8,128)S(1)} fusion(f32[512,64]{0,1:T(8,128)S(1)} %concatenate.13, f32[512,2048]{1,0:T(8,128)S(1)} %fusion.17, f32[512,2048]{1,0:T(8,128)S(1)} %fusion.8), kind=kOutput, calls=%fused_computation.1 | convolution fusion | flops 813694976 | bytes 9043968 | tf_op jit(solution)/shard_map/dot_general | solution.py:534
  135.3 10.9 %subtract_convert_fusion = bf16[2048,2048]{1,0:T(8,128)(2,1)} fusion(bf16[2048,2048]{1,0:T(8,128)(2,1)} %param.14, f32[512,2048]{1,0:T(8,128)} %copy-done.3, f32[512,2048]{1,0:T(8,128)S(1)} %fusion.8), kind=kOutput, calls=%fused_computation | convolution fusion | flops 4319084544 | bytes 25165824 | tf_op jit(solution)/shard_map/dot_general | solution.py:524
  146.2 27.8 %sum_everywhere.1 = f32[128,8,128]{2,1,0:T(8,128)S(1)} custom-call(f32[128,8,128]{2,1,0:T(8,128)S(1)} %bitcast.37), custom_call_target="tpu_custom_call" | custom-call | tf_op jit(solution)/shard_map/sum_everywhere/pallas_call | solution.py:439
  174.0 0.1 copy.30
  174.2 0.2 copy.29
  174.4 0.1 reshape.88
  174.5 0.2 reduce_sum.30
  174.6 0.1 reshape_subtract_fusion
  174.7 0.1 maximum_bitcast_fusion
  174.8 0.9 fusion.7
  (11 shorter events, 0.1 us)
Async XLA Ops:
  8.0 101.5 %copy-start = (f32[69,2048]{1,0:T(8,128)S(1)}, f32[69,2048]{1,0:T(8,128)}, u32[]{:S(2)}) copy-start(f32[69,2048]{1,0:T(8,128)} %param.13) | copy-start | bytes 1695748
  8.0 101.5 %copy-start.1 = (f32[512]{0:T(512)S(1)}, f32[512]{0:T(512)}, u32[]{:S(2)}) copy-start(f32[512]{0:T(512)} %param.11) | copy-start | bytes 6148
  109.6 3.6 %copy-start.2 = (f32[2048]{0:T(1024)S(1)}, f32[2048]{0:T(1024)}, u32[]{:S(2)}) copy-start(f32[2048]{0:T(1024)} %param.15) | copy-start | bytes 24580
  122.5 8.7 %copy-start.3 = (f32[512,2048]{1,0:T(8,128)}, f32[512,2048]{1,0:T(8,128)S(1)}, u32[]{:S(2)}) copy-start(f32[512,2048]{1,0:T(8,128)S(1)} %get-tuple-element.11) | copy-start | bytes 12582916

commit v3 on v2

--- a/solution.py
+++ b/solution.py
@@ -34,10 +34,31 @@
     return at(here, xl=tile // 16, y=(tile // 4) % 4, z=tile % 4)
 
 
+def dot(a, b):
+    return lax.dot_general(a, b, (((1,), (0,)), ((), ())), preferred_element_type=jnp.float32)
+
+
+def dot_turned(a, b):
+    return lax.dot_general(a, b, (((1,), (1,)), ((), ())), preferred_element_type=jnp.float32)
+
+
+def two_parts(x):
+    high = x.astype(jnp.bfloat16)
+    return high, (x - high.astype(jnp.float32)).astype(jnp.bfloat16)
+
+
+def dot_parts(x, order):
+    high, low = two_parts(x)
+    return dot(high, order) + dot(low, order)
+
+
 def solve_kernel(
-    field_ref, class_ref, table_ref, steep_ref, pick_ref, target_ref,
-    raw, rows_own, halo_up, halo_dn, class_up, class_dn, kappa, wide_a, wide_b, sent, got,
-    load_sem, halo_send, halo_recv, class_send, class_recv, out_send, out_recv, keep_sem,
+    field_ref, class_ref, table_ref, steep_ref, pick_ref,
+    onehot_ref, steep_all_ref, input_ref, near_ref, far_ref, bias_ref, weight_ref,
+    misfit_ref, turned_ref, part_ref,
+    raw, rows_own, halo_up, halo_dn, class_up, class_dn, kappa, wide_a, wide_b, picked, sent, got,
+    weight, hidden, turned, gain, pred, misfit, misfit_far, grad,
+    load_sem, halo_send, halo_recv, class_send, class_recv, out_send, out_recv, keep_sem, weight_sem,
 ):
     here = place()
     runs = rows_own.shape[1]
@@ -68,6 +89,8 @@
     for k in range(CHUNKS):
         for copy in load(k):
             copy.start()
+    weight_load = pltpu.make_async_copy(weight_ref, weight, weight_sem)
+    weight_load.start()
 
     barrier = pltpu.get_barrier_semaphore()
     for _, mate in mates:
@@ -135,20 +158,32 @@
         halo_dn[...] = jnp.zeros_like(halo_dn)
         class_dn[...] = jnp.full_like(class_dn, -1)
 
-    for k in range(CHUNKS):
+    first = lax.broadcasted_iota(jnp.int32, (width, width), 0)
+    second = lax.broadcasted_iota(jnp.int32, (width, width), 1)
+    blocks = width // 128
+    order = jnp.where(first == (second % 128) * blocks + second // 128, 1.0, 0.0)
+    order = order.astype(jnp.bfloat16)
+    lines = part * tile_rows
+
+    def prepare(k, none):
         for copy in load(k):
             copy.wait()
+        span = pl.ds(pl.multiple_of(k * lines, lines), lines)
+        lined = jnp.concatenate([raw[c, span] for c in range(blocks)], axis=1)
+        lined = dot_parts(lined, order)
+        for c in range(blocks):
+            raw[c, span] = lined[:, 128 * c : 128 * c + 128]
 
         def turn(j, carry):
             first = pl.multiple_of(j * SUB, SUB)
             for i in range(tile_rows):
-                for c in range(width // 128):
+                for c in range(blocks):
                     rows_own[i, pl.ds(first, SUB), pl.ds(128 * c, 128)] = raw[
                         c, pl.ds(j * (SUB * tile_rows) + i, SUB, stride=tile_rows), :
                     ]
             return carry
 
-        lax.fori_loop(k * part // SUB, (k + 1) * part // SUB, turn, 0)
+        lax.fori_loop(k * (part // SUB), (k + 1) * (part // SUB), turn, 0)
 
         @pl.when(has_up)
         def _():
@@ -158,6 +193,10 @@
         def _():
             halo_copy(k, False).start()
 
+        return none
+
+    lax.fori_loop(0, CHUNKS, prepare, 0)
+
     @pl.when(has_up)
     def _():
         class_copy(False).wait_recv()
@@ -168,13 +207,24 @@
 
     keep_up = jnp.where(has_up, 1.0, 0.0).astype(jnp.float32)
     keep_dn = jnp.where(has_dn, 1.0, 0.0).astype(jnp.float32)
-    lane = lax.broadcasted_iota(jnp.int32, (SUB, width), 1)
-    left, right = lane == 0, lane == width - 1
+    lane = lax.broadcasted_iota(jnp.int32, (SUB, 128), 1)
+    left, right = lane == 0, lane == 127
+    edge = width - 128
+
+    def next_column(x):
+        turned = jnp.where(right, 0.0, pltpu.roll(x[:, :128], 127, 1))
+        return jnp.concatenate([x[:, 128:], turned], axis=1)
+
+    def last_column(x, outermost):
+        turned = jnp.where(left, outermost[:, :128], pltpu.roll(x[:, edge:], 1, 1))
+        return jnp.concatenate([turned, x[:, :edge]], axis=1)
+
     span_rows = tile_rows + 2 * STEPS
 
-    def advance(s, carry):
-        first = pl.multiple_of(s * SUB, SUB)
+    def advance(k, half_chunk):
+        first = pl.multiple_of(k * part + half_chunk * SUB, SUB)
         runs_here = pl.ds(first, SUB)
+        picked_here = pl.ds(pl.multiple_of(half_chunk * SUB, SUB), SUB)
         steep = jnp.broadcast_to(steep_ref[runs_here, 0:1], (SUB, width))
         rest = 1.0 - steep
         pick = jnp.broadcast_to(pick_ref[runs_here, 0:1], (SUB, width))
@@ -222,10 +272,8 @@
                 below = row(i + 1)
                 below_spread = spread_of(i + 1, below)
                 flow_out = (spread + below_spread) * (below - centre)
-                beyond = jnp.where(right, 0.0, pltpu.roll(centre, width - 1, 1))
-                beyond_spread = jnp.where(right, 0.0, pltpu.roll(spread, width - 1, 1))
-                flow = (spread + beyond_spread) * (beyond - centre)
-                back = jnp.where(left, spread * centre, pltpu.roll(flow, 1, 1))
+                flow = (spread + next_column(spread)) * (next_column(centre) - centre)
+                back = last_column(flow, spread * centre)
                 total = centre + (flow_out - flow_in) + (flow - back)
                 if i < STEPS:
                     total = total * keep_up
@@ -234,15 +282,15 @@
                 if sink is not None:
                     sink[i] = total
                 if STEPS <= i < STEPS + tile_rows:
-                    owner, inner = (i - STEPS) // 4, (i - STEPS) % 4
-                    columns = pl.ds(inner * width, width)
                     if step > 0:
-                        total = jnp.where(pick == step + 1, total, sent[owner, runs_here, columns])
-                    sent[owner, runs_here, columns] = total
+                        total = jnp.where(pick == step + 1, total, picked[i - STEPS, picked_here])
+                    picked[i - STEPS, picked_here] = total
                 flow_in, centre, spread = flow_out, below, below_spread
-        return carry
-
-    for k in range(CHUNKS):
+
+    back_order = jnp.where(second == (first % 128) * blocks + first // 128, 1.0, 0.0)
+    back_order = back_order.astype(jnp.bfloat16)
+
+    def one_chunk(k, none):
         @pl.when(has_up)
         def _():
             halo_copy(k, False).wait_recv()
@@ -251,26 +299,124 @@
         def _():
             halo_copy(k, True).wait_recv()
 
-        lax.fori_loop(k * part // SUB, (k + 1) * part // SUB, advance, 0)
+        def half_of(half_chunk, carry):
+            advance(k, half_chunk)
+            return carry
+
+        lax.fori_loop(0, part // SUB, half_of, 0)
+        lined = dot_parts(picked[...].reshape(tile_rows * part, width), back_order)
+        span = pl.ds(pl.multiple_of(k * part, part), part)
+        for i in range(tile_rows):
+            sent[i // 4, span, pl.ds((i % 4) * width, width)] = lined[i * part : (i + 1) * part]
         for j in range(3):
             out_copy(k, j).start()
-
-    def keep(j):
-        if j == 3:
-            source, owner = sent.at[group], group
-        else:
-            source, owner = got.at[j], mates[j][0]
-        return pltpu.make_async_copy(
-            source, target_ref.at[pl.ds(pl.multiple_of(owner * runs, runs), runs)], keep_sem.at[j]
-        )
-
-    keep(3).start()
-    for j in range(3):
-        for k in range(CHUNKS):
-            out_copy(k, j).wait_recv()
-        keep(j).start()
-    for j in range(4):
-        keep(j).wait()
+        return none
+
+    lax.fori_loop(0, CHUNKS, one_chunk, 0)
+
+    cells = weight.shape[1]
+    hid = weight.shape[0]
+    all_runs = hidden.shape[0]
+    block = 256
+    f32, bf16 = jnp.float32, jnp.bfloat16
+    eye = lax.broadcasted_iota(jnp.int32, (block, block), 0) == lax.broadcasted_iota(
+        jnp.int32, (block, block), 1
+    )
+    eye = jnp.where(eye, 1.0, 0.0).astype(bf16)
+    share = 2.0 / all_runs
+
+    def hidden_block(n, none):
+        span = pl.ds(pl.multiple_of(n * block, block), block)
+        value = input_ref[:, span]
+        high, low = two_parts(value)
+        rest = (value - high.astype(f32) - low.astype(f32)).astype(bf16)
+        onehot = onehot_ref[...]
+        pre = dot(onehot, high) + (dot(onehot, low) + dot(onehot, rest))
+        pre = pre + steep_all_ref[...] * value[value.shape[0] - 1 :, :]
+        logistic = 1.0 / (1.0 + jnp.exp(-pre))
+        active = (pre * logistic).astype(bf16)
+        hidden[:, span] = active
+        gain[:, span] = logistic * (1.0 + pre * (1.0 - logistic)) * share
+        turned[span, :] = dot_turned(eye, active).astype(bf16)
+        return none
+
+    lax.fori_loop(0, hid // block, hidden_block, 0)
+    turned_copy = pltpu.make_async_copy(turned, turned_ref, keep_sem.at[0])
+    turned_copy.start()
+    weight_load.wait()
+
+    def pred_block(n, none):
+        span = pl.ds(pl.multiple_of(n * block, block), block)
+        pred[:, span] = dot(hidden[...], weight[:, span]) + bias_ref[:, span]
+        return none
+
+    lax.fori_loop(0, cells // block, pred_block, 0)
+
+    def compare(source, group_at, start, count, copy_row):
+        def some(b, none):
+            inner = pl.multiple_of(start + b * 16, 16)
+            at_run = pl.ds(pl.multiple_of(group_at * runs + inner, 16), 16)
+            value = (pred[at_run] - source[pl.ds(inner, 16)]).astype(bf16)
+            misfit[at_run] = value
+            if copy_row is not None:
+                misfit_far[pl.ds(pl.multiple_of(copy_row + b * 16, 16), 16)] = value
+            return none
+
+        lax.fori_loop(0, count // 16, some, 0)
+
+    for k in range(CHUNKS):
+        out_copy(k, 0).wait_recv()
+    compare(sent.at[group], group, 0, runs, None)
+    compare(got.at[0], mates[0][0], 0, runs, None)
+    near = pl.ds(pl.multiple_of(here["xh"] * (2 * runs), 2 * runs), 2 * runs)
+    far = (1 - here["xh"]) * (2 * runs)
+
+    def near_block(n, none):
+        span = pl.ds(pl.multiple_of(n * block, block), block)
+        back = dot_turned(misfit[near], weight[span, :]) * gain[near, span]
+        high, low = two_parts(back)
+        grad[:, span] = dot(near_ref[here["xh"]], high) + dot(near_ref[here["xh"]], low)
+        return none
+
+    lax.fori_loop(0, hid // block, near_block, 0)
+    near_copy = pltpu.make_async_copy(misfit.at[near], misfit_ref.at[near], keep_sem.at[1])
+    near_copy.start()
+
+    half = runs // 2
+    for h in range(2):
+        for k in range(h * CHUNKS // 2, (h + 1) * CHUNKS // 2):
+            out_copy(k, 1).wait_recv()
+            out_copy(k, 2).wait_recv()
+        for j in (1, 2):
+            at_row = here["core"] if j == 1 else 1 - here["core"]
+            compare(got.at[j], mates[j][0], h * half, half, at_row * half)
+
+        def far_block(n, none):
+            span = pl.ds(pl.multiple_of(n * block, block), block)
+            factor = jnp.concatenate(
+                [
+                    gain[pl.ds(pl.multiple_of(far + g * runs + h * half, half), half), span]
+                    for g in range(2)
+                ],
+                axis=0,
+            )
+            back = dot_turned(misfit_far[...], weight[span, :]) * factor
+            high, low = two_parts(back)
+            mix = far_ref[1 - here["xh"], h]
+            grad[:, span] += dot(mix, high) + dot(mix, low)
+            return none
+
+        lax.fori_loop(0, hid // block, far_block, 0)
+
+    far_span = pl.ds(pl.multiple_of(far, 2 * runs), 2 * runs)
+    far_copy = pltpu.make_async_copy(misfit.at[far_span], misfit_ref.at[far_span], keep_sem.at[2])
+    far_copy.start()
+    for i in range(part_ref.shape[0]):
+        r, c = i // (hid // 128), i % (hid // 128)
+        part_ref[i] = grad[8 * r : 8 * r + 8, 128 * c : 128 * c + 128]
+    turned_copy.wait()
+    near_copy.wait()
+    far_copy.wait()
     for k in range(CHUNKS):
         for j in range(3):
             out_copy(k, j).wait_send()
@@ -288,18 +434,27 @@
             halo_copy(k, False).wait_send()
 
 
-def solve(field, classes, table, steep, pick):
+def solve(field, classes, table, steep, pick, onehot, steepness, input_layer, near, far, bias, weight):
     runs, rows, width = field.shape
-    f32 = jnp.float32
+    hid, cells = weight.shape
+    all_runs = onehot.shape[0]
+    f32, bf16 = jnp.float32, jnp.bfloat16
     dma = pltpu.SemaphoreType.DMA
     vmem = pl.BlockSpec(memory_space=pltpu.VMEM)
     anywhere = pl.BlockSpec(memory_space=pl.ANY)
+    classes = classes.reshape(rows, 128, width // 128).transpose(0, 2, 1).reshape(rows, width)
     wide = jnp.broadcast_to(classes[:, None, :], (rows, SUB, width))
+    span = rows + 2 * STEPS
+    part = runs // CHUNKS
     return pl.pallas_call(
         solve_kernel,
-        out_shape=jax.ShapeDtypeStruct((4 * runs, 4 * width), f32),
-        in_specs=[anywhere, vmem, vmem, vmem, vmem],
-        out_specs=anywhere,
+        out_shape=(
+            jax.ShapeDtypeStruct((all_runs, cells), bf16),
+            jax.ShapeDtypeStruct((hid, all_runs), bf16),
+            jax.ShapeDtypeStruct((hid // 16, 8, 128), f32),
+        ),
+        in_specs=[anywhere] + [vmem] * 10 + [anywhere],
+        out_specs=(anywhere, anywhere, vmem),
         scratch_shapes=[
             pltpu.VMEM((width // 128, runs * rows, 128), f32),
             pltpu.VMEM((rows, runs, width), f32),
@@ -307,11 +462,20 @@
             pltpu.VMEM((STEPS, runs, width), f32),
             pltpu.VMEM((STEPS, SUB, width), jnp.int32),
             pltpu.VMEM((STEPS, SUB, width), jnp.int32),
-            pltpu.VMEM((rows + 2 * STEPS, SUB, width), f32),
-            pltpu.VMEM((rows + 2 * STEPS, SUB, width), f32),
-            pltpu.VMEM((rows + 2 * STEPS, SUB, width), f32),
+            pltpu.VMEM((span, SUB, width), f32),
+            pltpu.VMEM((span, SUB, width), f32),
+            pltpu.VMEM((span, SUB, width), f32),
+            pltpu.VMEM((rows, part, width), f32),
             pltpu.VMEM((4, runs, 4 * width), f32),
             pltpu.VMEM((3, runs, 4 * width), f32),
+            pltpu.VMEM((hid, cells), bf16),
+            pltpu.VMEM((all_runs, hid), bf16),
+            pltpu.VMEM((hid, all_runs), bf16),
+            pltpu.VMEM((all_runs, hid), f32),
+            pltpu.VMEM((all_runs, cells), f32),
+            pltpu.VMEM((all_runs, cells), bf16),
+            pltpu.VMEM((runs, cells), bf16),
+            pltpu.VMEM((64, hid), f32),
             dma((CHUNKS, 4)),
             dma((CHUNKS, 2)),
             dma((CHUNKS, 2)),
@@ -319,13 +483,66 @@
             dma((2,)),
             dma((CHUNKS, 3)),
             dma((CHUNKS, 3)),
-            dma((4,)),
+            dma((3,)),
+            dma,
         ],
         compiler_params=pltpu.CompilerParams(
-            collective_id=1, has_side_effects=True, vmem_limit_bytes=48 * MIB
+            collective_id=1, has_side_effects=True, vmem_limit_bytes=58 * MIB
         ),
         name="solve",
-    )(field.reshape(runs * rows, width), wide, table, steep, pick)
+    )(
+        field.reshape(runs * rows, width), wide, table, steep, pick,
+        onehot, steepness, input_layer, near, far, bias, weight,
+    )
+
+
+def update_kernel(turned_ref, misfit_ref, weight_ref, bias_ref, next_ref, misfit_out_ref, bias_out_ref):
+    f32, bf16 = jnp.float32, jnp.bfloat16
+    step = 1.0 / misfit_ref.shape[0]
+    block = 256
+
+    def columns(n, none):
+        span = pl.ds(pl.multiple_of(n * block, block), block)
+        grad = dot(turned_ref[...], misfit_ref[:, span])
+        next_ref[:, span] = (weight_ref[:, span].astype(f32) - step * grad).astype(bf16)
+        return none
+
+    lax.fori_loop(0, misfit_ref.shape[1] // block, columns, 0)
+    rows = misfit_out_ref.shape[0]
+    here = pl.multiple_of(pl.program_id(0) * rows, rows)
+    value = misfit_ref[pl.ds(here, rows)]
+    misfit_out_ref[...] = value
+
+    @pl.when(pl.program_id(0) == 0)
+    def _():
+        bias_out_ref[...] = bias_ref[...]
+
+    bias_out_ref[...] -= step * jnp.sum(value.astype(f32), axis=0, keepdims=True)
+
+
+def update(turned, misfit, weight, bias):
+    hid, cells = weight.shape
+    runs = misfit.shape[0]
+    steps = 8
+    whole = pl.BlockSpec((runs, cells), lambda i: (0, 0))
+    line = pl.BlockSpec((1, cells), lambda i: (0, 0))
+    tile = pl.BlockSpec((hid // steps, cells), lambda i: (i, 0))
+    return pl.pallas_call(
+        update_kernel,
+        grid=(steps,),
+        out_shape=(
+            jax.ShapeDtypeStruct(weight.shape, weight.dtype),
+            jax.ShapeDtypeStruct(misfit.shape, misfit.dtype),
+            jax.ShapeDtypeStruct(bias.shape, bias.dtype),
+        ),
+        in_specs=[pl.BlockSpec((hid // steps, runs), lambda i: (i, 0)), whole, tile, line],
+        out_specs=(tile, pl.BlockSpec((runs // steps, cells), lambda i: (i, 0)), line),
+        compiler_params=pltpu.CompilerParams(vmem_limit_bytes=40 * MIB),
+        cost_estimate=pl.CostEstimate(
+            flops=2 * hid * cells * runs, bytes_accessed=4 * hid * cells, transcendentals=0
+        ),
+        name="update",
+    )(turned, misfit, weight, bias)
 
 
 def sum_kernel(
@@ -454,92 +671,72 @@
     )(part)
 
 
-def features(run_levels, step_pick, steepness):
+def onehots(run_levels, step_pick):
     count = run_levels.shape[0]
-    onehot = (run_levels[:, :, None] == jnp.arange(LEVELS, dtype=jnp.int32)[None, None, :]).astype(
-        jnp.float32
-    )
-    onehot = onehot.reshape(count, -1)
-    moment = (step_pick[:, None] == jnp.arange(1, STEPS + 1, dtype=jnp.int32)[None, :]).astype(
-        jnp.float32
-    )
-    return jnp.concatenate([onehot, moment, steepness[:, None]], axis=1)
+    onehot = (run_levels[:, :, None] == jnp.arange(LEVELS, dtype=jnp.int32)).reshape(count, -1)
+    moment = step_pick[:, None] == jnp.arange(1, STEPS + 2, dtype=jnp.int32)
+    return jnp.concatenate([onehot, moment], axis=1).astype(jnp.bfloat16)
 
 
 def independent(run_levels, step_pick, steepness):
+    f32, bf16 = jnp.float32, jnp.bfloat16
     count = run_levels.shape[0]
-    f32 = jnp.float32
-    onehot = (run_levels[:, :, None] == jnp.arange(LEVELS - 1, dtype=jnp.int32)).astype(f32)
-    moment = (step_pick[:, None] == jnp.arange(1, STEPS, dtype=jnp.int32)).astype(f32)
+    level = jnp.arange(LEVELS - 1, dtype=jnp.int32)
+    onehot = (run_levels.T[:, None, :] == level[None, :, None]).reshape(-1, count)
+    moment = step_pick[None, :] == jnp.arange(1, STEPS, dtype=jnp.int32)[:, None]
+    high = lax.reduce_precision(steepness, 8, 7)
+    middle = lax.reduce_precision(steepness - high, 8, 7)
+    low = steepness - high - middle
     return jnp.concatenate(
         [
-            onehot.reshape(count, -1),
-            moment,
-            steepness[:, None],
-            jnp.ones((count, 1), f32),
-            jnp.zeros((count, 3), f32),
+            onehot.astype(bf16),
+            moment.astype(bf16),
+            jnp.ones((1, count), bf16),
+            jnp.stack([high, middle, low, jnp.zeros_like(low)]).astype(bf16),
+            jnp.zeros((64 - CLASSES * (LEVELS - 1) - STEPS - 4, count), bf16),
         ],
-        axis=1,
+        axis=0,
     )
 
 
 def all_features(sums):
     width = sums.shape[1]
-    classes = sums[: CLASSES * (LEVELS - 1)].reshape(CLASSES, LEVELS - 1, width)
     first = CLASSES * (LEVELS - 1)
+    classes = sums[:first].reshape(CLASSES, LEVELS - 1, width)
     moment = sums[first : first + STEPS - 1]
-    steep = sums[first + STEPS - 1 : first + STEPS]
-    ones = sums[first + STEPS : first + STEPS + 1]
+    ones = sums[first + STEPS - 1 : first + STEPS]
+    steep = jnp.sum(sums[first + STEPS : first + STEPS + 3], axis=0, keepdims=True)
     last = ones[None] - jnp.sum(classes, axis=1, keepdims=True)
     classes = jnp.concatenate([classes, last], axis=1).reshape(CLASSES * LEVELS, width)
     final = ones - jnp.sum(moment, axis=0, keepdims=True)
     return jnp.concatenate([classes, moment, final, steep], axis=0)
 
 
-def dsilu(pre):
-    logistic = jax.nn.sigmoid(pre)
-    return logistic * (1.0 + pre * (1.0 - logistic))
-
-
 def on_device(
     start_field, class_ids, run_levels, steepness, step_pick, input_layer, output_layer, output_bias
 ):
     local_runs = start_field.shape[0]
+    total_runs = run_levels.shape[0]
     first_run = lax.axis_index(GRP) * local_runs
     levels_here = lax.dynamic_slice_in_dim(run_levels, first_run, local_runs, 0)
     steep = lax.dynamic_slice_in_dim(steepness, first_run, local_runs, 0)[:, None]
     pick_here = lax.dynamic_slice_in_dim(step_pick, first_run, local_runs, 0)[:, None]
     table = 0.015 * jnp.exp(levels_here.astype(jnp.float32) * jnp.log(jnp.float32(1.35)))
-    target = solve(start_field, class_ids, table, steep, pick_here)
-    runs_total = target.shape[0]
-    feats = features(run_levels, step_pick, steepness)
-    pre = jnp.dot(feats, input_layer, precision=lax.Precision.HIGHEST)
-    hidden = jax.nn.silu(pre).astype(jnp.bfloat16)
-    error = (
-        jnp.dot(hidden, output_layer, preferred_element_type=jnp.float32)
-        + output_bias[None, :]
-        - target
-    )
-    slope = (error * (2.0 / runs_total)).astype(jnp.bfloat16)
-    grad = lax.dot_general(
-        hidden, slope, (((0,), (0,)), ((), ())), preferred_element_type=jnp.float32
-    )
-    output_next = (output_layer.astype(jnp.float32) - 0.5 * grad).astype(jnp.bfloat16)
-    bias_next = output_bias - 0.5 * jnp.sum(slope.astype(jnp.float32), axis=0)
-    gain_slope = dsilu(pre)
-    partial_back = lax.dot_general(
-        slope, output_layer, (((1,), (1,)), ((), ())), preferred_element_type=jnp.float32
-    )
     basis = independent(run_levels, step_pick, steepness)
-    partial_in = lax.dot_general(
-        basis, partial_back * gain_slope, (((0,), (0,)), ((), ())), precision=lax.Precision.HIGHEST
-    )
-    width = partial_in.shape[1]
-    tiles = partial_in.reshape(8, 8, width // 128, 128).transpose(0, 2, 1, 3).reshape(-1, 8, 128)
+    near = basis.reshape(64, 2, total_runs // 2).transpose(1, 0, 2)
+    far = basis.reshape(64, 2, 2, 2, local_runs // 2).transpose(1, 3, 0, 2, 4)
+    far = far.reshape(2, 2, 64, local_runs)
+    bias = output_bias[None, :]
+    misfit, turned, tiles = solve(
+        start_field, class_ids, table, steep, pick_here,
+        onehots(run_levels, step_pick), steepness[:, None], input_layer, near, far, bias, output_layer,
+    )
     tiles = sum_everywhere(tiles)
+    width = input_layer.shape[1]
     sums = tiles.reshape(8, width // 128, 8, 128).transpose(0, 2, 1, 3).reshape(64, width)
     input_next = input_layer - 2.0 * all_features(sums)
-    return (error.astype(jnp.bfloat16), output_next, bias_next, input_next)
+    output_next, misfit, bias_next = update(turned, misfit, output_layer, bias)
+    return (misfit, output_next, bias_next[0], input_next)
 
 
 def solution(mesh):

time: 176 us -> 154 us (0.88)
  matrix products: 35.9 us -> 0 us
  local copies, waits for them, and re-layouts: 4.63 us -> 18.5 us
    dot_general x5 -> x0, matrix products: 35.9 us -> none  [the longest x1 10.9 us: on_device(): lax.dot_general(hidden, slope, (((0,), (0,)), ((), ())), preferred_elemen...]
    pallas_call x1 -> x2, Pallas kernels: 102 us -> 86.3 us  [the longest x1 69.1 us: solve(): pl.pallas_call(solve_kernel, out_shape=(jax.ShapeDtypeStruct((all_runs, c...]
    pallas_call x1, Pallas kernels: 27.8 us -> 42.4 us  [sum_everywhere(): pl.pallas_call(sum_kernel, out_shape=jax.ShapeDtypeStruct(part.shape, f32...]
    unnamed x9 -> x21, local copies, waits for them, and re-layouts: 0.19 us -> 7.68 us
    eq x6 -> x11, local copies, waits for them, and re-layouts: 0.92 us -> 2.77 us  [the longest x5 1.06 us: independent(): run_levels.T[:, None, :] == level[None, :, None]]
where the time goes in v3:
time: 154 us; the launch traced here: 153 us
  Pallas kernels  129 us (84%)
  local copies, waits for them, and re-layouts  18.5 us (12%)
  other arithmetic  5.35 us (3%)
    pallas_call x1, Pallas kernels, solve(): pl.pallas_call(solve_kernel, out_shape=(jax.ShapeDtypeStruct((all_runs, c...  69.1 us
    pallas_call x1, Pallas kernels, sum_everywhere(): pl.pallas_call(sum_kernel, out_shape=jax.ShapeDtypeStruct(part.shape, f32...  42.4 us
    pallas_call x1, Pallas kernels, update(): pl.pallas_call(update_kernel, grid=(steps,), out_shape=(jax.ShapeDtypeStr...  17.2 us
    unnamed x21, local copies, waits for them, and re-layouts  7.68 us

profile of v3, /device:TPU:1, one launch (start us, length us, event | category | flops | bytes accessed | tf_op | source)
XLA Modules:
  0.0 153.4 jit_solution(12286888459879680827)
XLA Ops:
  0.6 0.0 copy-start.6
  0.6 0.9 copy.42
  1.5 0.1 copy.43
  1.6 0.8 broadcast_in_dim.41.class_ref
  2.4 0.7 multiply_exponential_fusion
  3.1 0.1 copy.45
  3.2 0.6 broadcast_multiply_fusion.table_ref
  3.8 0.8 dynamic-slice_bitcast_fusion.1
  4.6 0.7 copy.53.steep_ref
  5.3 0.8 dynamic-slice_bitcast_fusion
  6.1 0.7 copy.54.pick_ref
  6.8 0.8 broadcast_compare_fusion.1
  7.6 0.7 broadcast_bitcast_fusion
  8.3 0.1 copy.46
  8.5 0.1 eq.93
  8.6 0.8 add_convert_fusion.onehot_ref
  9.4 1.5 copy.55.steep_all_ref
  10.9 0.7 eq.99
  11.7 0.1 eq.100
  11.8 0.1 eq.102
  11.9 0.1 fusion.2
  11.9 0.7 eq.105
  12.6 0.1 compare_convert_fusion.2
  12.7 0.7 fusion.3
  13.5 1.2 concatenate.23
  14.7 0.2 eq.109
  14.9 0.2 fusion.1
  15.1 0.0 copy-done.6
  15.1 0.1 eq.112
  15.2 0.1 constant_dynamic-update-slice_fusion.5
  15.2 0.1 stack.19
  15.3 0.1 stack.20
  15.4 0.1 stack.21
  15.5 0.1 copy.52
  15.6 0.7 reshape.148.far_ref
  16.4 0.0 copy-start.2
  16.4 69.1 %solve.1 = (bf16[512,2048]{1,0:T(8,128)(2,1)}, bf16[2048,512]{1,0:T(8,128)(2,1)}, f32[128,8,128]{2,1,0:T(8,128)}) custom-call(f32[2048,512]{1,0:T(8,128)} %bitcast.41, s32[16,8,512]{2,1,0:T(8,128)} %broadcast_in_dim.41.class_ref, f32[128,8]{1,0:T(8,128)} %broadcast_multiply_fusion.table_ref, f32[128,1]{1,0:T(8,128)} %copy.53.steep_ref, ...), custom_call_target="tpu_custom_call" | custom-call | tf_op jit(solution)/shard_map/solve/pallas_call | solution.py:449
  85.5 0.0 copy-done.2
  85.5 0.0 copy-start
  85.5 3.4 %copy-done = bf16[2048,2048]{1,0:T(8,128)(2,1)S(1)} copy-done((bf16[2048,2048]{1,0:T(8,128)(2,1)S(1)}, bf16[2048,2048]{1,0:T(8,128)(2,1)}, u32[]{:S(2)}) %copy-start) | copy-done | bytes 8388632
  88.9 0.0 copy-start.3
  88.9 1.6 %copy-done.3 = bf16[512,2048]{1,0:T(8,128)(2,1)S(1)} copy-done((bf16[512,2048]{1,0:T(8,128)(2,1)S(1)}, bf16[512,2048]{1,0:T(8,128)(2,1)}, u32[]{:S(2)}) %copy-start.3) | copy-done | bytes 2097176
  90.4 0.0 copy-start.4
  90.4 1.6 %copy-done.4 = bf16[2048,512]{1,0:T(8,128)(2,1)S(1)} copy-done((bf16[2048,512]{1,0:T(8,128)(2,1)S(1)}, bf16[2048,512]{1,0:T(8,128)(2,1)}, u32[]{:S(2)}) %copy-start.4) | copy-done | bytes 2097176
  92.0 0.0 copy-start.1
  92.0 17.2 %update.1 = (bf16[2048,2048]{1,0:T(8,128)(2,1)}, bf16[512,2048]{1,0:T(8,128)(2,1)}, f32[1,2048]{1,0:T(1,128)}) custom-call(bf16[2048,512]{1,0:T(8,128)(2,1)S(1)} %copy-done.4, bf16[512,2048]{1,0:T(8,128)(2,1)S(1)} %copy-done.3, bf16[2048,2048]{1,0:T(8,128)(2,1)S(1)} %copy-done, f32[1,2048]{1,0:T(1,128)S(1)} %bitcast.38), custom_call_target="tpu_custom_call" | custom-call | flops 4294967296 | bytes 16777216 | tf_op jit(solution)/shard_map/update/pallas_call | solution.py:530
  109.3 0.0 copy-start.5
  109.3 0.0 copy-done.1
  109.3 42.4 %sum_everywhere.1 = f32[128,8,128]{2,1,0:T(8,128)S(1)} custom-call(f32[128,8,128]{2,1,0:T(8,128)S(1)} %copy-done.1), custom_call_target="tpu_custom_call" | custom-call | tf_op jit(solution)/shard_map/sum_everywhere/pallas_call | solution.py:656
  151.7 0.1 copy.66
  151.8 0.2 copy.65
  152.0 0.1 reshape.150
  152.1 0.2 reduce_sum.29
  152.3 0.1 reshape_subtract_fusion
  152.3 0.1 maximum_bitcast_fusion
  152.5 0.0 copy-done.5
  152.5 0.9 fusion
  (19 shorter events, 0.3 us)
Async XLA Ops:
  0.6 14.4 %copy-start.6 = (s32[512]{0:T(512)S(1)}, s32[512]{0:T(512)}, u32[]{:S(2)}) copy-start(s32[512]{0:T(512)} %param.12) | copy-start | bytes 6148
  16.4 69.1 %copy-start.2 = (f32[2048]{0:T(1024)S(1)}, f32[2048]{0:T(1024)}, u32[]{:S(2)}) copy-start(f32[2048]{0:T(1024)} %param.15) | copy-start | bytes 24580
  85.5 3.4 %copy-start = (bf16[2048,2048]{1,0:T(8,128)(2,1)S(1)}, bf16[2048,2048]{1,0:T(8,128)(2,1)}, u32[]{:S(2)}) copy-start(bf16[2048,2048]{1,0:T(8,128)(2,1)} %weight_ref.3) | copy-start | bytes 25165828
  88.9 1.6 %copy-start.3 = (bf16[512,2048]{1,0:T(8,128)(2,1)S(1)}, bf16[512,2048]{1,0:T(8,128)(2,1)}, u32[]{:S(2)}) copy-start(bf16[512,2048]{1,0:T(8,128)(2,1)} %get-tuple-element.11.misfit_ref) | copy-start | bytes 6291460
  90.4 1.6 %copy-start.4 = (bf16[2048,512]{1,0:T(8,128)(2,1)S(1)}, bf16[2048,512]{1,0:T(8,128)(2,1)}, u32[]{:S(2)}) copy-start(bf16[2048,512]{1,0:T(8,128)(2,1)} %get-tuple-element.10.turned_ref) | copy-start | bytes 6291460
  92.0 17.2 %copy-start.1 = (f32[128,8,128]{2,1,0:T(8,128)S(1)}, f32[128,8,128]{2,1,0:T(8,128)}, u32[]{:S(2)}) copy-start(f32[128,8,128]{2,1,0:T(8,128)} %get-tuple-element.15.part_ref) | copy-start | bytes 1572868
  109.3 43.2 %copy-start.5 = (f32[69,2048]{1,0:T(8,128)S(1)}, f32[69,2048]{1,0:T(8,128)}, u32[]{:S(2)}) copy-start(f32[69,2048]{1,0:T(8,128)} %input_ref.1) | copy-start | bytes 1695748

commit v4 on v3

--- a/solution.py
+++ b/solution.py
@@ -1,4 +1,4 @@
-import functools
+import math
 
 import jax
 import jax.numpy as jnp
@@ -53,12 +53,12 @@
 
 
 def solve_kernel(
-    field_ref, class_ref, table_ref, steep_ref, pick_ref,
-    onehot_ref, steep_all_ref, input_ref, near_ref, far_ref, bias_ref, weight_ref,
+    field_ref, ids_ref, about_ref, input_ref, bias_ref, weight_ref,
     misfit_ref, turned_ref, part_ref,
-    raw, rows_own, halo_up, halo_dn, class_up, class_dn, kappa, wide_a, wide_b, picked, sent, got,
-    weight, hidden, turned, gain, pred, misfit, misfit_far, grad,
+    raw, rows_own, class_ref, halo_up, halo_dn, class_up, class_dn, kappa, wide_a, wide_b, picked, sent, got,
+    relay, weight, hidden, turned, gain, pred, misfit, misfit_far, grad,
     load_sem, halo_send, halo_recv, class_send, class_recv, out_send, out_recv, keep_sem, weight_sem,
+    relay_send, relay_recv,
 ):
     here = place()
     runs = rows_own.shape[1]
@@ -104,7 +104,30 @@
     def _():
         pl.semaphore_signal(barrier, inc=1, device_id=dn, device_id_type=BY_ID)
 
+    xl = here["xl"]
+    ends_dn, ends_up = tile == 15, tile == 16
+    corner = 3 * (1 - xl)
+    relay_path = (here["y"] - corner + 4) % 4
+    is_relay = (here["z"] == corner) & (relay_path > 0)
+    relay_from = at(here, y=corner)
+    relay_to = at(here, xl=1 - xl, y=3 * xl, z=3 * xl)
+
+    @pl.when(is_relay)
+    def _():
+        for other in (relay_from, relay_to):
+            pl.semaphore_signal(barrier, inc=1, device_id=other, device_id_type=BY_ID)
+
+    @pl.when(ends_dn | ends_up)
+    def _():
+        for side in range(2):
+            for p in range(1, 4):
+                edge_at = 3 * (1 - side)
+                other = at(here, xl=side, y=(edge_at + p) % 4, z=edge_at)
+                pl.semaphore_signal(barrier, inc=1, device_id=other, device_id_type=BY_ID)
+
     callers = 3 + jnp.where(has_up, 1, 0) + jnp.where(has_dn, 1, 0)
+    callers = callers + jnp.where(is_relay, 2, 0)
+    callers = callers + jnp.where(ends_dn | ends_up, 6, 0)
     pl.semaphore_wait(barrier, callers)
 
     def class_copy(upward):
@@ -127,6 +150,39 @@
             device_id=up if upward else dn,
             device_id_type=BY_ID,
         )
+
+    def detour_copy(k, upward):
+        span = pl.ds(pl.multiple_of(k * part, part), part)
+        return pltpu.make_async_remote_copy(
+            src_ref=rows_own.at[pl.ds(0 if upward else tile_rows - STEPS, STEPS), span],
+            dst_ref=relay.at[k // 4],
+            send_sem=halo_send.at[k, 0 if upward else 1],
+            recv_sem=relay_recv.at[k // 4],
+            device_id=at(here, y=(here["y"] + k % 4) % 4),
+            device_id_type=BY_ID,
+        )
+
+    def forward_copy(k, upward):
+        span = pl.ds(pl.multiple_of(k * part, part), part)
+        return pltpu.make_async_remote_copy(
+            src_ref=relay.at[k // 4],
+            dst_ref=(halo_dn if upward else halo_up).at[:, span],
+            send_sem=relay_send.at[k // 4],
+            recv_sem=halo_recv.at[k, 0 if upward else 1],
+            device_id=relay_to,
+            device_id_type=BY_ID,
+        )
+
+    def send_halo(k, upward):
+        detour = (ends_up if upward else ends_dn) & (k % 4 > 0)
+
+        @pl.when((has_up if upward else has_dn) & jnp.logical_not(detour))
+        def _():
+            halo_copy(k, upward).start()
+
+        @pl.when(detour)
+        def _():
+            detour_copy(k, upward).start()
 
     def out_copy(k, j):
         span = pl.ds(pl.multiple_of(k * part, part), part)
@@ -140,23 +196,15 @@
             device_id_type=BY_ID,
         )
 
-    @pl.when(has_up)
-    def _():
-        class_copy(True).start()
-
-    @pl.when(has_dn)
-    def _():
-        class_copy(False).start()
-
     @pl.when(jnp.logical_not(has_up))
     def _():
         halo_up[...] = jnp.zeros_like(halo_up)
-        class_up[...] = jnp.full_like(class_up, -1)
+        class_up[...] = jnp.full_like(class_up, -1.0)
 
     @pl.when(jnp.logical_not(has_dn))
     def _():
         halo_dn[...] = jnp.zeros_like(halo_dn)
-        class_dn[...] = jnp.full_like(class_dn, -1)
+        class_dn[...] = jnp.full_like(class_dn, -1.0)
 
     first = lax.broadcasted_iota(jnp.int32, (width, width), 0)
     second = lax.broadcasted_iota(jnp.int32, (width, width), 1)
@@ -164,6 +212,17 @@
     order = jnp.where(first == (second % 128) * blocks + second // 128, 1.0, 0.0)
     order = order.astype(jnp.bfloat16)
     lines = part * tile_rows
+    class_rows = dot(ids_ref[...].astype(jnp.float32).astype(jnp.bfloat16), order)
+    for i in range(tile_rows):
+        class_ref[i] = jnp.broadcast_to(class_rows[i : i + 1], (SUB, width))
+
+    @pl.when(has_up)
+    def _():
+        class_copy(True).start()
+
+    @pl.when(has_dn)
+    def _():
+        class_copy(False).start()
 
     def prepare(k, none):
         for copy in load(k):
@@ -185,14 +244,8 @@
 
         lax.fori_loop(k * (part // SUB), (k + 1) * (part // SUB), turn, 0)
 
-        @pl.when(has_up)
-        def _():
-            halo_copy(k, True).start()
-
-        @pl.when(has_dn)
-        def _():
-            halo_copy(k, False).start()
-
+        send_halo(k, True)
+        send_halo(k, False)
         return none
 
     lax.fori_loop(0, CHUNKS, prepare, 0)
@@ -225,12 +278,12 @@
         first = pl.multiple_of(k * part + half_chunk * SUB, SUB)
         runs_here = pl.ds(first, SUB)
         picked_here = pl.ds(pl.multiple_of(half_chunk * SUB, SUB), SUB)
-        steep = jnp.broadcast_to(steep_ref[runs_here, 0:1], (SUB, width))
+        about = about_ref[pl.ds(pl.multiple_of(group * runs + first, SUB), SUB)]
+        table = 0.015 * jnp.exp(about[:, :CLASSES] * math.log(1.35))
+        steep = jnp.broadcast_to(about[:, CLASSES : CLASSES + 1], (SUB, width))
+        pick = jnp.broadcast_to(about[:, CLASSES + 1 : CLASSES + 2], (SUB, width))
         rest = 1.0 - steep
-        pick = jnp.broadcast_to(pick_ref[runs_here, 0:1], (SUB, width))
-        half = [
-            jnp.broadcast_to(table_ref[runs_here, c : c + 1], (SUB, width)) for c in range(CLASSES)
-        ]
+        half = [jnp.broadcast_to(table[:, c : c + 1], (SUB, width)) for c in range(CLASSES)]
         for i in range(span_rows):
             if i < STEPS:
                 klass = class_up[i]
@@ -240,7 +293,7 @@
                 klass = class_dn[i - STEPS - tile_rows]
             value = jnp.zeros((SUB, width), jnp.float32)
             for c in range(CLASSES):
-                value = jnp.where(klass == c, half[c], value)
+                value = jnp.where(klass == float(c), half[c], value)
             kappa[i] = value
 
         def start_row(i):
@@ -283,7 +336,7 @@
                     sink[i] = total
                 if STEPS <= i < STEPS + tile_rows:
                     if step > 0:
-                        total = jnp.where(pick == step + 1, total, picked[i - STEPS, picked_here])
+                        total = jnp.where(pick == step + 1.0, total, picked[i - STEPS, picked_here])
                     picked[i - STEPS, picked_here] = total
                 flow_in, centre, spread = flow_out, below, below_spread
 
@@ -291,6 +344,15 @@
     back_order = back_order.astype(jnp.bfloat16)
 
     def one_chunk(k, none):
+        for upward in (False, True):
+            for slot in range(2):
+                @pl.when(is_relay & (xl == int(upward)) & (k == 2 * slot))
+                def _():
+                    passed = relay_path + 4 * slot
+                    forward = forward_copy(passed, upward)
+                    detour_copy(passed, upward).wait_recv()
+                    forward.start()
+
         @pl.when(has_up)
         def _():
             halo_copy(k, False).wait_recv()
@@ -324,15 +386,52 @@
     )
     eye = jnp.where(eye, 1.0, 0.0).astype(bf16)
     share = 2.0 / all_runs
+    about = about_ref[...]
+    steep_all = about[:, CLASSES : CLASSES + 1]
+    feats = input_ref.shape[0]
+    onehots = CLASSES * LEVELS
+    entry = lax.broadcasted_iota(jnp.int32, (16, feats), 0)
+    column = lax.broadcasted_iota(jnp.int32, (16, feats), 1)
+    source = jnp.where(column < onehots, column // LEVELS, CLASSES + 1)
+    spread_out = dot(about.astype(bf16), jnp.where(entry == source, 1.0, 0.0).astype(bf16))
+    column = lax.broadcasted_iota(jnp.int32, (all_runs, feats), 1)
+    wanted = jnp.where(column < onehots, column % LEVELS, column - onehots + 1)
+    wanted = jnp.where(column < onehots + STEPS, wanted, -1).astype(f32)
+    onehot = jnp.where(spread_out == wanted, 1.0, 0.0).astype(bf16)
+
+    def independent(rows):
+        count = rows.shape[0]
+        kept = LEVELS - 1
+        levels_end, moments_end = CLASSES * kept, CLASSES * kept + STEPS - 1
+        high, middle = two_parts(rows)
+        low = (rows - high.astype(f32) - middle.astype(f32)).astype(bf16)
+        line = lax.broadcasted_iota(jnp.int32, (64, 16), 0)
+        entry = lax.broadcasted_iota(jnp.int32, (64, 16), 1)
+        source = jnp.where(line < levels_end, line // kept, CLASSES + 1)
+        source = jnp.where(line > moments_end, CLASSES, source)
+
+        def chosen(last, extra):
+            keep = (entry == source) & ((line < last) | (line == extra))
+            return jnp.where(keep, 1.0, 0.0).astype(bf16)
+
+        value = (
+            dot_turned(chosen(moments_end, moments_end + 1), high)
+            + dot_turned(chosen(0, moments_end + 2), middle)
+            + dot_turned(chosen(0, moments_end + 3), low)
+        )
+        line = lax.broadcasted_iota(jnp.int32, (64, count), 0)
+        wanted = jnp.where(line < levels_end, line % kept, line - levels_end + 1).astype(f32)
+        marks = jnp.where(value == wanted, 1.0, 0.0)
+        value = jnp.where(line < moments_end, marks, value)
+        return jnp.where(line == moments_end, 1.0, value).astype(bf16)
 
     def hidden_block(n, none):
         span = pl.ds(pl.multiple_of(n * block, block), block)
         value = input_ref[:, span]
         high, low = two_parts(value)
         rest = (value - high.astype(f32) - low.astype(f32)).astype(bf16)
-        onehot = onehot_ref[...]
         pre = dot(onehot, high) + (dot(onehot, low) + dot(onehot, rest))
-        pre = pre + steep_all_ref[...] * value[value.shape[0] - 1 :, :]
+        pre = pre + steep_all * value[value.shape[0] - 1 :, :]
         logistic = 1.0 / (1.0 + jnp.exp(-pre))
         active = (pre * logistic).astype(bf16)
         hidden[:, span] = active
@@ -371,11 +470,13 @@
     near = pl.ds(pl.multiple_of(here["xh"] * (2 * runs), 2 * runs), 2 * runs)
     far = (1 - here["xh"]) * (2 * runs)
 
+    near_mix = independent(about_ref[near])
+
     def near_block(n, none):
         span = pl.ds(pl.multiple_of(n * block, block), block)
         back = dot_turned(misfit[near], weight[span, :]) * gain[near, span]
         high, low = two_parts(back)
-        grad[:, span] = dot(near_ref[here["xh"]], high) + dot(near_ref[here["xh"]], low)
+        grad[:, span] = dot(near_mix, high) + dot(near_mix, low)
         return none
 
     lax.fori_loop(0, hid // block, near_block, 0)
@@ -391,18 +492,14 @@
             at_row = here["core"] if j == 1 else 1 - here["core"]
             compare(got.at[j], mates[j][0], h * half, half, at_row * half)
 
+        far_rows = [pl.ds(pl.multiple_of(far + g * runs + h * half, half), half) for g in range(2)]
+        mix = independent(jnp.concatenate([about_ref[rows] for rows in far_rows], axis=0))
+
         def far_block(n, none):
             span = pl.ds(pl.multiple_of(n * block, block), block)
-            factor = jnp.concatenate(
-                [
-                    gain[pl.ds(pl.multiple_of(far + g * runs + h * half, half), half), span]
-                    for g in range(2)
-                ],
-                axis=0,
-            )
+            factor = jnp.concatenate([gain[rows, span] for rows in far_rows], axis=0)
             back = dot_turned(misfit_far[...], weight[span, :]) * factor
             high, low = two_parts(back)
-            mix = far_ref[1 - here["xh"], h]
             grad[:, span] += dot(mix, high) + dot(mix, low)
             return none
 
@@ -414,6 +511,11 @@
     for i in range(part_ref.shape[0]):
         r, c = i // (hid // 128), i % (hid // 128)
         part_ref[i] = grad[8 * r : 8 * r + 8, 128 * c : 128 * c + 128]
+    @pl.when(is_relay)
+    def _():
+        for slot in range(2):
+            forward_copy(relay_path + 4 * slot, False).wait_send()
+
     turned_copy.wait()
     near_copy.wait()
     far_copy.wait()
@@ -434,16 +536,14 @@
             halo_copy(k, False).wait_send()
 
 
-def solve(field, classes, table, steep, pick, onehot, steepness, input_layer, near, far, bias, weight):
+def solve(field, classes, about, input_layer, bias, weight):
     runs, rows, width = field.shape
     hid, cells = weight.shape
-    all_runs = onehot.shape[0]
+    all_runs = about.shape[0]
     f32, bf16 = jnp.float32, jnp.bfloat16
     dma = pltpu.SemaphoreType.DMA
     vmem = pl.BlockSpec(memory_space=pltpu.VMEM)
     anywhere = pl.BlockSpec(memory_space=pl.ANY)
-    classes = classes.reshape(rows, 128, width // 128).transpose(0, 2, 1).reshape(rows, width)
-    wide = jnp.broadcast_to(classes[:, None, :], (rows, SUB, width))
     span = rows + 2 * STEPS
     part = runs // CHUNKS
     return pl.pallas_call(
@@ -453,21 +553,23 @@
             jax.ShapeDtypeStruct((hid, all_runs), bf16),
             jax.ShapeDtypeStruct((hid // 16, 8, 128), f32),
         ),
-        in_specs=[anywhere] + [vmem] * 10 + [anywhere],
+        in_specs=[anywhere] + [vmem] * 4 + [anywhere],
         out_specs=(anywhere, anywhere, vmem),
         scratch_shapes=[
             pltpu.VMEM((width // 128, runs * rows, 128), f32),
             pltpu.VMEM((rows, runs, width), f32),
+            pltpu.VMEM((rows, SUB, width), f32),
             pltpu.VMEM((STEPS, runs, width), f32),
             pltpu.VMEM((STEPS, runs, width), f32),
-            pltpu.VMEM((STEPS, SUB, width), jnp.int32),
-            pltpu.VMEM((STEPS, SUB, width), jnp.int32),
+            pltpu.VMEM((STEPS, SUB, width), f32),
+            pltpu.VMEM((STEPS, SUB, width), f32),
             pltpu.VMEM((span, SUB, width), f32),
             pltpu.VMEM((span, SUB, width), f32),
             pltpu.VMEM((span, SUB, width), f32),
             pltpu.VMEM((rows, part, width), f32),
             pltpu.VMEM((4, runs, 4 * width), f32),
             pltpu.VMEM((3, runs, 4 * width), f32),
+            pltpu.VMEM((2, STEPS, part, width), f32),
             pltpu.VMEM((hid, cells), bf16),
             pltpu.VMEM((all_runs, hid), bf16),
             pltpu.VMEM((hid, all_runs), bf16),
@@ -485,14 +587,15 @@
             dma((CHUNKS, 3)),
             dma((3,)),
             dma,
+            dma((2,)),
+            dma((2,)),
         ],
         compiler_params=pltpu.CompilerParams(
             collective_id=1, has_side_effects=True, vmem_limit_bytes=58 * MIB
         ),
         name="solve",
     )(
-        field.reshape(runs * rows, width), wide, table, steep, pick,
-        onehot, steepness, input_layer, near, far, bias, weight,
+        field.reshape(runs * rows, width), classes, about, input_layer, bias, weight,
     )
 
 
@@ -507,7 +610,7 @@
         next_ref[:, span] = (weight_ref[:, span].astype(f32) - step * grad).astype(bf16)
         return none
 
-    lax.fori_loop(0, misfit_ref.shape[1] // block, columns, 0)
+    lax.fori_loop(0, misfit_ref.shape[1] // block, columns, 0, unroll=True)
     rows = misfit_out_ref.shape[0]
     here = pl.multiple_of(pl.program_id(0) * rows, rows)
     value = misfit_ref[pl.ds(here, rows)]
@@ -523,7 +626,7 @@
 def update(turned, misfit, weight, bias):
     hid, cells = weight.shape
     runs = misfit.shape[0]
-    steps = 8
+    steps = 4
     whole = pl.BlockSpec((runs, cells), lambda i: (0, 0))
     line = pl.BlockSpec((1, cells), lambda i: (0, 0))
     tile = pl.BlockSpec((hid // steps, cells), lambda i: (i, 0))
@@ -537,7 +640,7 @@
         ),
         in_specs=[pl.BlockSpec((hid // steps, runs), lambda i: (i, 0)), whole, tile, line],
         out_specs=(tile, pl.BlockSpec((runs // steps, cells), lambda i: (i, 0)), line),
-        compiler_params=pltpu.CompilerParams(vmem_limit_bytes=40 * MIB),
+        compiler_params=pltpu.CompilerParams(vmem_limit_bytes=60 * MIB),
         cost_estimate=pl.CostEstimate(
             flops=2 * hid * cells * runs, bytes_accessed=4 * hid * cells, transcendentals=0
         ),
@@ -671,34 +774,6 @@
     )(part)
 
 
-def onehots(run_levels, step_pick):
-    count = run_levels.shape[0]
-    onehot = (run_levels[:, :, None] == jnp.arange(LEVELS, dtype=jnp.int32)).reshape(count, -1)
-    moment = step_pick[:, None] == jnp.arange(1, STEPS + 2, dtype=jnp.int32)
-    return jnp.concatenate([onehot, moment], axis=1).astype(jnp.bfloat16)
-
-
-def independent(run_levels, step_pick, steepness):
-    f32, bf16 = jnp.float32, jnp.bfloat16
-    count = run_levels.shape[0]
-    level = jnp.arange(LEVELS - 1, dtype=jnp.int32)
-    onehot = (run_levels.T[:, None, :] == level[None, :, None]).reshape(-1, count)
-    moment = step_pick[None, :] == jnp.arange(1, STEPS, dtype=jnp.int32)[:, None]
-    high = lax.reduce_precision(steepness, 8, 7)
-    middle = lax.reduce_precision(steepness - high, 8, 7)
-    low = steepness - high - middle
-    return jnp.concatenate(
-        [
-            onehot.astype(bf16),
-            moment.astype(bf16),
-            jnp.ones((1, count), bf16),
-            jnp.stack([high, middle, low, jnp.zeros_like(low)]).astype(bf16),
-            jnp.zeros((64 - CLASSES * (LEVELS - 1) - STEPS - 4, count), bf16),
-        ],
-        axis=0,
-    )
-
-
 def all_features(sums):
     width = sums.shape[1]
     first = CLASSES * (LEVELS - 1)
@@ -715,22 +790,18 @@
 def on_device(
     start_field, class_ids, run_levels, steepness, step_pick, input_layer, output_layer, output_bias
 ):
-    local_runs = start_field.shape[0]
-    total_runs = run_levels.shape[0]
-    first_run = lax.axis_index(GRP) * local_runs
-    levels_here = lax.dynamic_slice_in_dim(run_levels, first_run, local_runs, 0)
-    steep = lax.dynamic_slice_in_dim(steepness, first_run, local_runs, 0)[:, None]
-    pick_here = lax.dynamic_slice_in_dim(step_pick, first_run, local_runs, 0)[:, None]
-    table = 0.015 * jnp.exp(levels_here.astype(jnp.float32) * jnp.log(jnp.float32(1.35)))
-    basis = independent(run_levels, step_pick, steepness)
-    near = basis.reshape(64, 2, total_runs // 2).transpose(1, 0, 2)
-    far = basis.reshape(64, 2, 2, 2, local_runs // 2).transpose(1, 3, 0, 2, 4)
-    far = far.reshape(2, 2, 64, local_runs)
+    f32 = jnp.float32
+    about = jnp.concatenate(
+        [
+            run_levels.astype(f32),
+            steepness[:, None],
+            step_pick[:, None].astype(f32),
+            jnp.zeros((run_levels.shape[0], 16 - CLASSES - 2), f32),
+        ],
+        axis=1,
+    )
     bias = output_bias[None, :]
-    misfit, turned, tiles = solve(
-        start_field, class_ids, table, steep, pick_here,
-        onehots(run_levels, step_pick), steepness[:, None], input_layer, near, far, bias, output_layer,
-    )
+    misfit, turned, tiles = solve(start_field, class_ids, about, input_layer, bias, output_layer)
     tiles = sum_everywhere(tiles)
     width = input_layer.shape[1]
     sums = tiles.reshape(8, width // 128, 8, 128).transpose(0, 2, 1, 3).reshape(64, width)

time: 154 us -> 122 us (0.79)
  local copies, waits for them, and re-layouts: 18.5 us -> 1.28 us
  Pallas kernels: 129 us -> 116 us
  other arithmetic: 5.35 us -> 3.44 us
    unnamed x21 -> x5, local copies, waits for them, and re-layouts: 7.68 us -> 0.17 us
    pallas_call x1, Pallas kernels: 42.4 us -> 35.6 us  [sum_everywhere(): pl.pallas_call(sum_kernel, out_shape=jax.ShapeDtypeStruct(part.shape, f32...]
    pallas_call x1, Pallas kernels: 17.2 us -> 11.5 us  [update(): pl.pallas_call(update_kernel, grid=(steps,), out_shape=(jax.ShapeDtypeStr...]
    broadcast_in_dim x7 -> x1, local copies, waits for them, and re-layouts: 5.26 us -> 0.01 us  [on_device(): jnp.zeros((run_levels.shape[0], 16 - CLASSES - 2), f32)]
    eq x11 -> x0, local copies, waits for them, and re-layouts: 2.77 us -> none  [the longest x5 1.06 us: independent(): run_levels.T[:, None, :] == level[None, :, None]]
where the time goes in v4:
time: 122 us
  Pallas kernels  116 us (95%)
  other arithmetic  3.44 us (3%)
  local copies, waits for them, and re-layouts  1.28 us (1%)
    pallas_call x1, Pallas kernels, solve(): pl.pallas_call(solve_kernel, out_shape=(jax.ShapeDtypeStruct((all_runs, c...  69.2 us
    pallas_call x1, Pallas kernels, sum_everywhere(): pl.pallas_call(sum_kernel, out_shape=jax.ShapeDtypeStruct(part.shape, f32...  35.6 us
    pallas_call x1, Pallas kernels, update(): pl.pallas_call(update_kernel, grid=(steps,), out_shape=(jax.ShapeDtypeStr...  11.5 us

profile of v4, /device:TPU:1, one launch (start us, length us, event | category | flops | bytes accessed | tf_op | source)
XLA Modules:
  0.0 121.7 jit_solution(18380207658202786563)
XLA Ops:
  0.6 0.7 convert_element_type.10
  1.3 0.7 convert_element_type.9
  2.0 0.1 pad.9.clone
  2.1 0.8 maximum_maximum_fusion
  2.9 0.8 copy.17.about_ref
  3.7 69.2 %solve.1 = (bf16[512,2048]{1,0:T(8,128)(2,1)}, bf16[2048,512]{1,0:T(8,128)(2,1)}, f32[128,8,128]{2,1,0:T(8,128)}) custom-call(f32[2048,512]{1,0:T(8,128)} %bitcast.24, s32[16,512]{1,0:T(8,128)} %ids_ref.1, f32[512,16]{1,0:T(8,128)} %copy.17.about_ref, f32[69,2048]{1,0:T(8,128)} %input_ref.1, f32[1,2048]{1,0:T(1,128)} %bitcast.31, bf16[2048,2048]{1,0:T(8,128)(2,1)} %weight_ref.3), custom_call_target="tpu_custom_call" | custom-call | tf_op jit(solution)/shard_map/solve/pallas_call | solution.py:549
  72.9 0.0 copy-start
  72.9 11.5 %update.1 = (bf16[2048,2048]{1,0:T(8,128)(2,1)}, bf16[512,2048]{1,0:T(8,128)(2,1)}, f32[1,2048]{1,0:T(1,128)}) custom-call(bf16[2048,512]{1,0:T(8,128)(2,1)} %get-tuple-element.10.turned_ref, bf16[512,2048]{1,0:T(8,128)(2,1)} %get-tuple-element.11.misfit_ref, bf16[2048,2048]{1,0:T(8,128)(2,1)} %weight_ref.3, f32[1,2048]{1,0:T(1,128)} %bitcast.32), custom_call_target="tpu_custom_call" | custom-call | flops 4294967296 | bytes 16777216 | tf_op jit(solution)/shard_map/update/pallas_call | solution.py:633
  84.4 0.0 copy-start.1
  84.4 0.0 copy-done
  84.4 35.6 %sum_everywhere.1 = f32[128,8,128]{2,1,0:T(8,128)S(1)} custom-call(f32[128,8,128]{2,1,0:T(8,128)S(1)} %copy-done), custom_call_target="tpu_custom_call" | custom-call | tf_op jit(solution)/shard_map/sum_everywhere/pallas_call | solution.py:759
  120.0 0.1 copy.23
  120.1 0.2 copy.22
  120.4 0.1 reshape.63
  120.5 0.2 reduce_sum.29
  120.6 0.1 reshape_subtract_fusion
  120.7 0.1 maximum_bitcast_fusion
  120.8 0.0 copy-done.1
  120.8 0.9 fusion
  (4 shorter events, 0.1 us)
Async XLA Ops:
  72.9 11.5 %copy-start = (f32[128,8,128]{2,1,0:T(8,128)S(1)}, f32[128,8,128]{2,1,0:T(8,128)}, u32[]{:S(2)}) copy-start(f32[128,8,128]{2,1,0:T(8,128)} %get-tuple-element.15.part_ref) | copy-start | bytes 1572868
  84.4 36.4 %copy-start.1 = (f32[69,2048]{1,0:T(8,128)S(1)}, f32[69,2048]{1,0:T(8,128)}, u32[]{:S(2)}) copy-start(f32[69,2048]{1,0:T(8,128)} %input_ref.1) | copy-start | bytes 1695748

commit v5 on v4

--- a/solution.py
+++ b/solution.py
@@ -54,11 +54,12 @@
 
 def solve_kernel(
     field_ref, ids_ref, about_ref, input_ref, bias_ref, weight_ref,
-    misfit_ref, turned_ref, part_ref,
+    misfit_ref, turned_ref, sums_ref,
     raw, rows_own, class_ref, halo_up, halo_dn, class_up, class_dn, kappa, wide_a, wide_b, picked, sent, got,
     relay, weight, hidden, turned, gain, pred, misfit, misfit_far, grad,
+    tiles, pair, own, landed, middle, landed_z, mine,
     load_sem, halo_send, halo_recv, class_send, class_recv, out_send, out_recv, keep_sem, weight_sem,
-    relay_send, relay_recv,
+    relay_send, relay_recv, sum_send, sum_recv,
 ):
     here = place()
     runs = rows_own.shape[1]
@@ -125,7 +126,22 @@
                 other = at(here, xl=side, y=(edge_at + p) % 4, z=edge_at)
                 pl.semaphore_signal(barrier, inc=1, device_id=other, device_id_type=BY_ID)
 
-    callers = 3 + jnp.where(has_up, 1, 0) + jnp.where(has_dn, 1, 0)
+    plane = here["xh"] * 8 + here["xl"] * 4 + here["y"]
+
+    def in_plane(k):
+        return at(here, xh=k // 8, xl=(k // 4) % 2, y=k % 4)
+
+    def greet(j, none):
+        other = in_plane((plane + j) % 16)
+        pl.semaphore_signal(barrier, inc=1, device_id=other, device_id_type=BY_ID)
+        return none
+
+    lax.fori_loop(1, 16, greet, 0)
+    for j in range(1, 4):
+        other = at(here, z=(here["z"] + j) % 4)
+        pl.semaphore_signal(barrier, inc=1, device_id=other, device_id_type=BY_ID)
+
+    callers = 3 + 18 + jnp.where(has_up, 1, 0) + jnp.where(has_dn, 1, 0)
     callers = callers + jnp.where(is_relay, 2, 0)
     callers = callers + jnp.where(ends_dn | ends_up, 6, 0)
     pl.semaphore_wait(barrier, callers)
@@ -384,8 +400,8 @@
     eye = lax.broadcasted_iota(jnp.int32, (block, block), 0) == lax.broadcasted_iota(
         jnp.int32, (block, block), 1
     )
-    eye = jnp.where(eye, 1.0, 0.0).astype(bf16)
     share = 2.0 / all_runs
+    eye = jnp.where(eye, -0.5 * share, 0.0).astype(bf16)
     about = about_ref[...]
     steep_all = about[:, CLASSES : CLASSES + 1]
     feats = input_ref.shape[0]
@@ -508,9 +524,74 @@
     far_span = pl.ds(pl.multiple_of(far, 2 * runs), 2 * runs)
     far_copy = pltpu.make_async_copy(misfit.at[far_span], misfit_ref.at[far_span], keep_sem.at[2])
     far_copy.start()
-    for i in range(part_ref.shape[0]):
+    for i in range(tiles.shape[0]):
         r, c = i // (hid // 128), i % (hid // 128)
-        part_ref[i] = grad[8 * r : 8 * r + 8, 128 * c : 128 * c + 128]
+        tiles[i] = grad[8 * r : 8 * r + 8, 128 * c : 128 * c + 128]
+
+    def sum_copy(stage, source, sink, device):
+        return pltpu.make_async_remote_copy(
+            src_ref=source,
+            dst_ref=sink,
+            send_sem=sum_send.at[stage],
+            recv_sem=sum_recv.at[stage],
+            device_id=device,
+            device_id_type=BY_ID,
+        )
+
+    core, z = here["core"], here["z"]
+    mate = at(here, core=1 - core)
+    share_of = 4
+    chips = own.shape[0]
+    swap = sum_copy(0, tiles.at[pl.ds((1 - core) * chips, chips)], pair, mate)
+    swap.start()
+    swap.wait_recv()
+    own[...] = tiles[pl.ds(core * chips, chips)] + pair[...]
+
+    def scatter(j, none):
+        other = (plane + j) % 16
+        sum_copy(
+            1,
+            own.at[pl.ds(other * share_of, share_of)],
+            landed.at[pl.ds((j - 1) * share_of, share_of)],
+            in_plane(other),
+        ).start()
+        return none
+
+    lax.fori_loop(1, 16, scatter, 0)
+    scattered = sum_copy(1, own.at[pl.ds(0, 15 * share_of)], landed, mate)
+    scattered.wait_recv()
+    total = own[pl.ds(plane * share_of, share_of)]
+    for j in range(15):
+        total = total + landed[j * share_of : (j + 1) * share_of]
+    middle[...] = total
+    for j in range(1, 4):
+        other = (z + j) % 4
+        sum_copy(2, middle.at[other], landed_z.at[j - 1], at(here, z=other)).start()
+    scattered_z = sum_copy(2, middle.at[pl.ds(0, 3)], landed_z, mate)
+    scattered_z.wait_recv()
+    mine[...] = middle[z] + (landed_z[0] + landed_z[1] + landed_z[2])
+    slot = core * chips + plane * share_of
+    sums_ref[slot + z] = mine[...]
+    for j in range(1, 4):
+        sum_copy(3, mine, sums_ref.at[slot + z], at(here, z=(z + j) % 4)).start()
+    gathered_z = sum_copy(3, middle.at[pl.ds(0, 3)], landed_z, mate)
+    gathered_z.wait_recv()
+    quad = pl.ds(slot, share_of)
+
+    def gather(j, none):
+        sum_copy(4, sums_ref.at[quad], sums_ref.at[quad], in_plane((plane + j) % 16)).start()
+        return none
+
+    lax.fori_loop(1, 16, gather, 0)
+    gathered = sum_copy(4, own.at[pl.ds(0, 15 * share_of)], landed, mate)
+    gathered.wait_recv()
+    half_sums = sums_ref.at[pl.ds(core * chips, chips)]
+    last = sum_copy(5, half_sums, half_sums, mate)
+    last.start()
+    last.wait()
+    for copy in (swap, scattered, scattered_z, gathered_z, gathered):
+        copy.wait_send()
+
     @pl.when(is_relay)
     def _():
         for slot in range(2):
@@ -578,6 +659,13 @@
             pltpu.VMEM((all_runs, cells), bf16),
             pltpu.VMEM((runs, cells), bf16),
             pltpu.VMEM((64, hid), f32),
+            pltpu.VMEM((hid // 16, 8, 128), f32),
+            pltpu.VMEM((hid // 32, 8, 128), f32),
+            pltpu.VMEM((hid // 32, 8, 128), f32),
+            pltpu.VMEM((60, 8, 128), f32),
+            pltpu.VMEM((4, 8, 128), f32),
+            pltpu.VMEM((3, 8, 128), f32),
+            pltpu.VMEM((8, 128), f32),
             dma((CHUNKS, 4)),
             dma((CHUNKS, 2)),
             dma((CHUNKS, 2)),
@@ -589,6 +677,8 @@
             dma,
             dma((2,)),
             dma((2,)),
+            dma((6,)),
+            dma((6,)),
         ],
         compiler_params=pltpu.CompilerParams(
             collective_id=1, has_side_effects=True, vmem_limit_bytes=58 * MIB
@@ -599,15 +689,18 @@
     )
 
 
-def update_kernel(turned_ref, misfit_ref, weight_ref, bias_ref, next_ref, misfit_out_ref, bias_out_ref):
+def update_kernel(
+    turned_ref, misfit_ref, weight_ref, bias_ref, sums_ref, input_ref,
+    next_ref, misfit_out_ref, bias_out_ref, input_out_ref,
+):
     f32, bf16 = jnp.float32, jnp.bfloat16
     step = 1.0 / misfit_ref.shape[0]
     block = 256
 
     def columns(n, none):
         span = pl.ds(pl.multiple_of(n * block, block), block)
-        grad = dot(turned_ref[...], misfit_ref[:, span])
-        next_ref[:, span] = (weight_ref[:, span].astype(f32) - step * grad).astype(bf16)
+        change = dot(turned_ref[...], misfit_ref[:, span])
+        next_ref[:, span] = (weight_ref[:, span].astype(f32) + change).astype(bf16)
         return none
 
     lax.fori_loop(0, misfit_ref.shape[1] // block, columns, 0, unroll=True)
@@ -619,16 +712,42 @@
     @pl.when(pl.program_id(0) == 0)
     def _():
         bias_out_ref[...] = bias_ref[...]
+        feats, hid = input_ref.shape
+        kept = LEVELS - 1
+        levels_end, moments_end = CLASSES * kept, CLASSES * kept + STEPS - 1
+        row = lax.broadcasted_iota(jnp.int32, (feats, 64), 0)
+        line = lax.broadcasted_iota(jnp.int32, (feats, 64), 1)
+        group = jnp.where(row < CLASSES * LEVELS, row // LEVELS, CLASSES)
+        inner = row - group * LEVELS
+        length = jnp.where(group < CLASSES, kept, STEPS - 1)
+        line_group = jnp.where(line < levels_end, line // kept, CLASSES)
+        line_inner = line - line_group * kept
+        same = (group == line_group) & (line < moments_end)
+        mix = jnp.where(same & (inner == line_inner), 1.0, 0.0)
+        mix = jnp.where(inner == length, jnp.where(same, -1.0, mix), mix)
+        mix = jnp.where((inner == length) & (line == moments_end), 1.0, mix)
+        steep = jnp.where((line > moments_end) & (line <= moments_end + 3), 1.0, 0.0)
+        mix = jnp.where(row == feats - 1, steep, mix).astype(bf16)
+        across = hid // 128
+        for c in range(across):
+            sums = jnp.concatenate([sums_ref[r * across + c] for r in range(8)], axis=0)
+            high, middle = two_parts(sums)
+            low = (sums - high.astype(f32) - middle.astype(f32)).astype(bf16)
+            grad = dot(mix, high) + (dot(mix, middle) + dot(mix, low))
+            span = slice(128 * c, 128 * c + 128)
+            input_out_ref[:, span] = input_ref[:, span] - 2.0 * grad
 
     bias_out_ref[...] -= step * jnp.sum(value.astype(f32), axis=0, keepdims=True)
 
 
-def update(turned, misfit, weight, bias):
+def update(turned, misfit, weight, bias, sums, input_layer):
     hid, cells = weight.shape
     runs = misfit.shape[0]
     steps = 4
     whole = pl.BlockSpec((runs, cells), lambda i: (0, 0))
     line = pl.BlockSpec((1, cells), lambda i: (0, 0))
+    layer = pl.BlockSpec(input_layer.shape, lambda i: (0, 0))
+    all_sums = pl.BlockSpec(sums.shape, lambda i: (0, 0, 0))
     tile = pl.BlockSpec((hid // steps, cells), lambda i: (i, 0))
     return pl.pallas_call(
         update_kernel,
@@ -637,15 +756,95 @@
             jax.ShapeDtypeStruct(weight.shape, weight.dtype),
             jax.ShapeDtypeStruct(misfit.shape, misfit.dtype),
             jax.ShapeDtypeStruct(bias.shape, bias.dtype),
+            jax.ShapeDtypeStruct(input_layer.shape, input_layer.dtype),
         ),
-        in_specs=[pl.BlockSpec((hid // steps, runs), lambda i: (i, 0)), whole, tile, line],
-        out_specs=(tile, pl.BlockSpec((runs // steps, cells), lambda i: (i, 0)), line),
+        in_specs=[pl.BlockSpec((hid // steps, runs), lambda i: (i, 0)), whole, tile, line, all_sums, layer],
+        out_specs=(tile, pl.BlockSpec((runs // steps, cells), lambda i: (i, 0)), line, layer),
         compiler_params=pltpu.CompilerParams(vmem_limit_bytes=60 * MIB),
         cost_estimate=pl.CostEstimate(
             flops=2 * hid * cells * runs, bytes_accessed=4 * hid * cells, transcendentals=0
         ),
         name="update",
-    )(turned, misfit, weight, bias)
+    )(turned, misfit, weight, bias, sums, input_layer)
+
+
+def update_kernel(
+    turned_ref, misfit_ref, weight_ref, bias_ref, sums_ref, input_ref,
+    next_ref, misfit_out_ref, bias_out_ref, input_out_ref,
+):
+    f32, bf16 = jnp.float32, jnp.bfloat16
+    step = 1.0 / misfit_ref.shape[0]
+    block = 256
+
+    def columns(n, none):
+        span = pl.ds(pl.multiple_of(n * block, block), block)
+        change = dot(turned_ref[...], misfit_ref[:, span])
+        next_ref[:, span] = (weight_ref[:, span].astype(f32) + change).astype(bf16)
+        return none
+
+    lax.fori_loop(0, misfit_ref.shape[1] // block, columns, 0, unroll=True)
+    rows = misfit_out_ref.shape[0]
+    here = pl.multiple_of(pl.program_id(0) * rows, rows)
+    value = misfit_ref[pl.ds(here, rows)]
+    misfit_out_ref[...] = value
+
+    @pl.when(pl.program_id(0) == 0)
+    def _():
+        bias_out_ref[...] = bias_ref[...]
+        feats, hid = input_ref.shape
+        kept = LEVELS - 1
+        levels_end, moments_end = CLASSES * kept, CLASSES * kept + STEPS - 1
+        row = lax.broadcasted_iota(jnp.int32, (feats, 64), 0)
+        line = lax.broadcasted_iota(jnp.int32, (feats, 64), 1)
+        group = jnp.where(row < CLASSES * LEVELS, row // LEVELS, CLASSES)
+        inner = row - group * LEVELS
+        length = jnp.where(group < CLASSES, kept, STEPS - 1)
+        line_group = jnp.where(line < levels_end, line // kept, CLASSES)
+        line_inner = line - line_group * kept
+        same = (group == line_group) & (line < moments_end)
+        mix = jnp.where(same & (inner == line_inner), 1.0, 0.0)
+        mix = jnp.where(inner == length, jnp.where(same, -1.0, mix), mix)
+        mix = jnp.where((inner == length) & (line == moments_end), 1.0, mix)
+        steep = jnp.where((line > moments_end) & (line <= moments_end + 3), 1.0, 0.0)
+        mix = jnp.where(row == feats - 1, steep, mix).astype(bf16)
+        across = hid // 128
+        for c in range(across):
+            sums = jnp.concatenate([sums_ref[r * across + c] for r in range(8)], axis=0)
+            high, middle = two_parts(sums)
+            low = (sums - high.astype(f32) - middle.astype(f32)).astype(bf16)
+            grad = dot(mix, high) + (dot(mix, middle) + dot(mix, low))
+            span = slice(128 * c, 128 * c + 128)
+            input_out_ref[:, span] = input_ref[:, span] - 2.0 * grad
+
+    bias_out_ref[...] -= step * jnp.sum(value.astype(f32), axis=0, keepdims=True)
+
+
+def update(turned, misfit, weight, bias, sums, input_layer):
+    hid, cells = weight.shape
+    runs = misfit.shape[0]
+    steps = 4
+    whole = pl.BlockSpec((runs, cells), lambda i: (0, 0))
+    line = pl.BlockSpec((1, cells), lambda i: (0, 0))
+    layer = pl.BlockSpec(input_layer.shape, lambda i: (0, 0))
+    all_sums = pl.BlockSpec(sums.shape, lambda i: (0, 0, 0))
+    tile = pl.BlockSpec((hid // steps, cells), lambda i: (i, 0))
+    return pl.pallas_call(
+        update_kernel,
+        grid=(steps,),
+        out_shape=(
+            jax.ShapeDtypeStruct(weight.shape, weight.dtype),
+            jax.ShapeDtypeStruct(misfit.shape, misfit.dtype),
+            jax.ShapeDtypeStruct(bias.shape, bias.dtype),
+            jax.ShapeDtypeStruct(input_layer.shape, input_layer.dtype),
+        ),
+        in_specs=[pl.BlockSpec((hid // steps, runs), lambda i: (i, 0)), whole, tile, line, all_sums, layer],
+        out_specs=(tile, pl.BlockSpec((runs // steps, cells), lambda i: (i, 0)), line, layer),
+        compiler_params=pltpu.CompilerParams(vmem_limit_bytes=60 * MIB),
+        cost_estimate=pl.CostEstimate(
+            flops=2 * hid * cells * runs, bytes_accessed=4 * hid * cells, transcendentals=0
+        ),
+        name="update",
+    )(turned, misfit, weight, bias, sums, input_layer)
 
 
 def sum_kernel(
@@ -774,19 +973,6 @@
     )(part)
 
 
-def all_features(sums):
-    width = sums.shape[1]
-    first = CLASSES * (LEVELS - 1)
-    classes = sums[:first].reshape(CLASSES, LEVELS - 1, width)
-    moment = sums[first : first + STEPS - 1]
-    ones = sums[first + STEPS - 1 : first + STEPS]
-    steep = jnp.sum(sums[first + STEPS : first + STEPS + 3], axis=0, keepdims=True)
-    last = ones[None] - jnp.sum(classes, axis=1, keepdims=True)
-    classes = jnp.concatenate([classes, last], axis=1).reshape(CLASSES * LEVELS, width)
-    final = ones - jnp.sum(moment, axis=0, keepdims=True)
-    return jnp.concatenate([classes, moment, final, steep], axis=0)
-
-
 def on_device(
     start_field, class_ids, run_levels, steepness, step_pick, input_layer, output_layer, output_bias
 ):
@@ -801,12 +987,10 @@
         axis=1,
     )
     bias = output_bias[None, :]
-    misfit, turned, tiles = solve(start_field, class_ids, about, input_layer, bias, output_layer)
-    tiles = sum_everywhere(tiles)
-    width = input_layer.shape[1]
-    sums = tiles.reshape(8, width // 128, 8, 128).transpose(0, 2, 1, 3).reshape(64, width)
-    input_next = input_layer - 2.0 * all_features(sums)
-    output_next, misfit, bias_next = update(turned, misfit, output_layer, bias)
+    misfit, turned, sums = solve(start_field, class_ids, about, input_layer, bias, output_layer)
+    output_next, misfit, bias_next, input_next = update(
+        turned, misfit, output_layer, bias, sums, input_layer
+    )
     return (misfit, output_next, bias_next[0], input_next)
 
 

time: 122 us -> 117 us (0.959)
  Pallas kernels: 116 us -> 113 us
  other arithmetic: 3.44 us -> 2.16 us
    pallas_call x1 -> x0, Pallas kernels: 35.6 us -> none  [sum_everywhere(): pl.pallas_call(sum_kernel, out_shape=jax.ShapeDtypeStruct(part.shape, f32...]
    pallas_call x1, Pallas kernels: 69.2 us -> 100 us  [solve(): pl.pallas_call(solve_kernel, out_shape=(jax.ShapeDtypeStruct((all_runs, c...]
where the time goes in v5:
time: 117 us
  Pallas kernels  113 us (97%)
  other arithmetic  2.16 us (2%)
    pallas_call x1, Pallas kernels, solve(): pl.pallas_call(solve_kernel, out_shape=(jax.ShapeDtypeStruct((all_runs, c...  100 us
    pallas_call x1, Pallas kernels, update(): pl.pallas_call(update_kernel, grid=(steps,), out_shape=(jax.ShapeDtypeStr...  12.5 us

profile of v5, /device:TPU:1, one launch (start us, length us, event | category | flops | bytes accessed | tf_op | source)
XLA Modules:
  0.0 116.6 jit_solution(11542693227377441598)
XLA Ops:
  0.6 0.1 pad.3.clone
  0.7 0.7 convert_element_type.10
  1.4 0.7 convert_element_type.9
  2.1 0.8 maximum_maximum_fusion
  2.9 0.8 copy.16.about_ref
  3.7 100.4 %solve.1 = (bf16[512,2048]{1,0:T(8,128)(2,1)}, bf16[2048,512]{1,0:T(8,128)(2,1)}, f32[128,8,128]{2,1,0:T(8,128)}) custom-call(f32[2048,512]{1,0:T(8,128)} %bitcast.5, s32[16,512]{1,0:T(8,128)} %ids_ref.1, f32[512,16]{1,0:T(8,128)} %copy.16.about_ref, f32[69,2048]{1,0:T(8,128)} %input_ref.3, f32[1,2048]{1,0:T(1,128)} %bitcast.7, bf16[2048,2048]{1,0:T(8,128)(2,1)} %weight_ref.3), custom_call_target="tpu_custom_call" | custom-call | tf_op jit(solution)/shard_map/solve/pallas_call | solution.py:630
  104.1 12.5 %update.1 = (bf16[2048,2048]{1,0:T(8,128)(2,1)}, bf16[512,2048]{1,0:T(8,128)(2,1)}, f32[1,2048]{1,0:T(1,128)}, f32[69,2048]{1,0:T(8,128)}) custom-call(bf16[2048,512]{1,0:T(8,128)(2,1)} %get-tuple-element.11.turned_ref, bf16[512,2048]{1,0:T(8,128)(2,1)} %get-tuple-element.12.misfit_ref, bf16[2048,2048]{1,0:T(8,128)(2,1)} %weight_ref.3, f32[1,2048]{1,0:T(1,128)} %bitcast.8, ...), custom_call_target="tpu_custom_call" | custom-call | flops 4294967296 | bytes 16777216 | tf_op jit(solution)/shard_map/update/pallas_call | solution.py:831
  (1 shorter events, 0.0 us)

commit v6 on v5

--- a/solution.py
+++ b/solution.py
@@ -53,9 +53,9 @@
 
 
 def solve_kernel(
-    field_ref, ids_ref, about_ref, input_ref, bias_ref, weight_ref,
+    field_ref, ids_ref, levels_ref, steep_ref, pick_ref, input_ref, bias_ref, weight_ref,
     misfit_ref, turned_ref, sums_ref,
-    raw, rows_own, class_ref, halo_up, halo_dn, class_up, class_dn, kappa, wide_a, wide_b, picked, sent, got,
+    about_ref, raw, rows_own, class_ref, halo_up, halo_dn, class_up, class_dn, kappa, wide_a, wide_b, picked, sent, got,
     relay, weight, hidden, turned, gain, pred, misfit, misfit_far, grad,
     tiles, pair, own, landed, middle, landed_z, mine,
     load_sem, halo_send, halo_recv, class_send, class_recv, out_send, out_recv, keep_sem, weight_sem,
@@ -228,6 +228,13 @@
     order = jnp.where(first == (second % 128) * blocks + second // 128, 1.0, 0.0)
     order = order.astype(jnp.bfloat16)
     lines = part * tile_rows
+    of_run = [
+        levels_ref[...].astype(jnp.float32),
+        steep_ref[...],
+        pick_ref[...].astype(jnp.float32),
+        jnp.zeros((128 - CLASSES - 2, about_ref.shape[0]), jnp.float32),
+    ]
+    about_ref[...] = jnp.concatenate(of_run, axis=0).T[:, : about_ref.shape[1]]
     class_rows = dot(ids_ref[...].astype(jnp.float32).astype(jnp.bfloat16), order)
     for i in range(tile_rows):
         class_ref[i] = jnp.broadcast_to(class_rows[i : i + 1], (SUB, width))
@@ -361,7 +368,7 @@
 
     def one_chunk(k, none):
         for upward in (False, True):
-            for slot in range(2):
+            for slot in range(CHUNKS // 4):
                 @pl.when(is_relay & (xl == int(upward)) & (k == 2 * slot))
                 def _():
                     passed = relay_path + 4 * slot
@@ -594,7 +601,7 @@
 
     @pl.when(is_relay)
     def _():
-        for slot in range(2):
+        for slot in range(CHUNKS // 4):
             forward_copy(relay_path + 4 * slot, False).wait_send()
 
     turned_copy.wait()
@@ -617,10 +624,10 @@
             halo_copy(k, False).wait_send()
 
 
-def solve(field, classes, about, input_layer, bias, weight):
+def solve(field, classes, levels, steep, pick, input_layer, bias, weight):
     runs, rows, width = field.shape
     hid, cells = weight.shape
-    all_runs = about.shape[0]
+    all_runs = levels.shape[1]
     f32, bf16 = jnp.float32, jnp.bfloat16
     dma = pltpu.SemaphoreType.DMA
     vmem = pl.BlockSpec(memory_space=pltpu.VMEM)
@@ -634,9 +641,10 @@
             jax.ShapeDtypeStruct((hid, all_runs), bf16),
             jax.ShapeDtypeStruct((hid // 16, 8, 128), f32),
         ),
-        in_specs=[anywhere] + [vmem] * 4 + [anywhere],
+        in_specs=[anywhere] + [vmem] * 6 + [anywhere],
         out_specs=(anywhere, anywhere, vmem),
         scratch_shapes=[
+            pltpu.VMEM((all_runs, 16), f32),
             pltpu.VMEM((width // 128, runs * rows, 128), f32),
             pltpu.VMEM((rows, runs, width), f32),
             pltpu.VMEM((rows, SUB, width), f32),
@@ -650,7 +658,7 @@
             pltpu.VMEM((rows, part, width), f32),
             pltpu.VMEM((4, runs, 4 * width), f32),
             pltpu.VMEM((3, runs, 4 * width), f32),
-            pltpu.VMEM((2, STEPS, part, width), f32),
+            pltpu.VMEM((CHUNKS // 4, STEPS, part, width), f32),
             pltpu.VMEM((hid, cells), bf16),
             pltpu.VMEM((all_runs, hid), bf16),
             pltpu.VMEM((hid, all_runs), bf16),
@@ -675,8 +683,8 @@
             dma((CHUNKS, 3)),
             dma((3,)),
             dma,
-            dma((2,)),
-            dma((2,)),
+            dma((CHUNKS // 4,)),
+            dma((CHUNKS // 4,)),
             dma((6,)),
             dma((6,)),
         ],
@@ -685,7 +693,7 @@
         ),
         name="solve",
     )(
-        field.reshape(runs * rows, width), classes, about, input_layer, bias, weight,
+        field.reshape(runs * rows, width), classes, levels, steep, pick, input_layer, bias, weight,
     )
 
 
@@ -976,18 +984,11 @@
 def on_device(
     start_field, class_ids, run_levels, steepness, step_pick, input_layer, output_layer, output_bias
 ):
-    f32 = jnp.float32
-    about = jnp.concatenate(
-        [
-            run_levels.astype(f32),
-            steepness[:, None],
-            step_pick[:, None].astype(f32),
-            jnp.zeros((run_levels.shape[0], 16 - CLASSES - 2), f32),
-        ],
-        axis=1,
+    bias = output_bias[None, :]
+    misfit, turned, sums = solve(
+        start_field, class_ids, run_levels.T, steepness[None, :], step_pick[None, :],
+        input_layer, bias, output_layer,
     )
-    bias = output_bias[None, :]
-    misfit, turned, sums = solve(start_field, class_ids, about, input_layer, bias, output_layer)
     output_next, misfit, bias_next, input_next = update(
         turned, misfit, output_layer, bias, sums, input_layer
     )

time: 117 us -> 114 us (0.974)
  other arithmetic: 2.16 us -> 0 us
    convert_element_type x2 -> x0, other arithmetic: 1.4 us -> none  [the longest x1 0.72 us: on_device(): run_levels.astype(f32)]
where the time goes in v6:
time: 114 us
  Pallas kernels  113 us (99%)
    pallas_call x1, Pallas kernels, solve(): pl.pallas_call(solve_kernel, out_shape=(jax.ShapeDtypeStruct((all_runs, c...  100 us
    pallas_call x1, Pallas kernels, update(): pl.pallas_call(update_kernel, grid=(steps,), out_shape=(jax.ShapeDtypeStr...  12.5 us

profile of v6, /device:TPU:1, one launch (start us, length us, event | category | flops | bytes accessed | tf_op | source)
XLA Modules:
  0.0 113.6 jit_solution(6580959492658584134)
XLA Ops:
  0.6 100.4 %solve.1 = (bf16[512,2048]{1,0:T(8,128)(2,1)}, bf16[2048,512]{1,0:T(8,128)(2,1)}, f32[128,8,128]{2,1,0:T(8,128)}) custom-call(f32[2048,512]{1,0:T(8,128)} %bitcast.6, s32[16,512]{1,0:T(8,128)} %ids_ref.1, s32[8,512]{1,0:T(8,128)} %bitcast.7, f32[1,512]{1,0:T(1,128)} %bitcast.10, s32[1,512]{1,0:T(1,128)} %bitcast.11, f32[69,2048]{1,0:T(8,128)} %input_ref.3, ...), custom_call_target="tpu_custom_call" | custom-call | tf_op jit(solution)/shard_map/solve/pallas_call | solution.py:637
  101.1 12.5 %update.1 = (bf16[2048,2048]{1,0:T(8,128)(2,1)}, bf16[512,2048]{1,0:T(8,128)(2,1)}, f32[1,2048]{1,0:T(1,128)}, f32[69,2048]{1,0:T(8,128)}) custom-call(bf16[2048,512]{1,0:T(8,128)(2,1)} %get-tuple-element.11.turned_ref, bf16[512,2048]{1,0:T(8,128)(2,1)} %get-tuple-element.12.misfit_ref, bf16[2048,2048]{1,0:T(8,128)(2,1)} %weight_ref.3, f32[1,2048]{1,0:T(1,128)} %bitcast.9, ...), custom_call_target="tpu_custom_call" | custom-call | flops 4294967296 | bytes 16777216 | tf_op jit(solution)/shard_map/update/pallas_call | solution.py:839

commit v7 on v6

--- a/solution.py
+++ b/solution.py
@@ -502,7 +502,7 @@
         grad[:, span] = dot(near_mix, high) + dot(near_mix, low)
         return none
 
-    lax.fori_loop(0, hid // block, near_block, 0)
+    lax.fori_loop(0, hid // block, near_block, 0, unroll=4)
     near_copy = pltpu.make_async_copy(misfit.at[near], misfit_ref.at[near], keep_sem.at[1])
     near_copy.start()
 
@@ -526,7 +526,7 @@
             grad[:, span] += dot(mix, high) + dot(mix, low)
             return none
 
-        lax.fori_loop(0, hid // block, far_block, 0)
+        lax.fori_loop(0, hid // block, far_block, 0, unroll=True)
 
     far_span = pl.ds(pl.multiple_of(far, 2 * runs), 2 * runs)
     far_copy = pltpu.make_async_copy(misfit.at[far_span], misfit_ref.at[far_span], keep_sem.at[2])

time: 114 us -> 113 us (level)
  no operation moved by 1% of the time
where the time goes in v7:
time: 113 us
  Pallas kernels  112 us (99%)
    pallas_call x1, Pallas kernels, solve(): pl.pallas_call(solve_kernel, out_shape=(jax.ShapeDtypeStruct((all_runs, c...  99.4 us
    pallas_call x1, Pallas kernels, update(): pl.pallas_call(update_kernel, grid=(steps,), out_shape=(jax.ShapeDtypeStr...  12.5 us

profile of v7, /device:TPU:1, one launch (start us, length us, event | category | flops | bytes accessed | tf_op | source)
XLA Modules:
  0.0 112.5 jit_solution(11684491817271689465)
XLA Ops:
  0.6 99.4 %solve.1 = (bf16[512,2048]{1,0:T(8,128)(2,1)}, bf16[2048,512]{1,0:T(8,128)(2,1)}, f32[128,8,128]{2,1,0:T(8,128)}) custom-call(f32[2048,512]{1,0:T(8,128)} %bitcast.6, s32[16,512]{1,0:T(8,128)} %ids_ref.1, s32[8,512]{1,0:T(8,128)} %bitcast.7, f32[1,512]{1,0:T(1,128)} %bitcast.10, s32[1,512]{1,0:T(1,128)} %bitcast.11, f32[69,2048]{1,0:T(8,128)} %input_ref.3, ...), custom_call_target="tpu_custom_call" | custom-call | tf_op jit(solution)/shard_map/solve/pallas_call | solution.py:637
  100.0 12.5 %update.1 = (bf16[2048,2048]{1,0:T(8,128)(2,1)}, bf16[512,2048]{1,0:T(8,128)(2,1)}, f32[1,2048]{1,0:T(1,128)}, f32[69,2048]{1,0:T(8,128)}) custom-call(bf16[2048,512]{1,0:T(8,128)(2,1)} %get-tuple-element.11.turned_ref, bf16[512,2048]{1,0:T(8,128)(2,1)} %get-tuple-element.12.misfit_ref, bf16[2048,2048]{1,0:T(8,128)(2,1)} %weight_ref.3, f32[1,2048]{1,0:T(1,128)} %bitcast.9, ...), custom_call_target="tpu_custom_call" | custom-call | flops 4294967296 | bytes 16777216 | tf_op jit(solution)/shard_map/update/pallas_call | solution.py:839

commit v8 on v7

--- a/solution.py
+++ b/solution.py
@@ -723,8 +723,8 @@
         feats, hid = input_ref.shape
         kept = LEVELS - 1
         levels_end, moments_end = CLASSES * kept, CLASSES * kept + STEPS - 1
-        row = lax.broadcasted_iota(jnp.int32, (feats, 64), 0)
-        line = lax.broadcasted_iota(jnp.int32, (feats, 64), 1)
+        row = lax.broadcasted_iota(jnp.int32, (feats, 192), 0)
+        line = lax.broadcasted_iota(jnp.int32, (feats, 192), 1) % 64
         group = jnp.where(row < CLASSES * LEVELS, row // LEVELS, CLASSES)
         inner = row - group * LEVELS
         length = jnp.where(group < CLASSES, kept, STEPS - 1)
@@ -737,12 +737,18 @@
         steep = jnp.where((line > moments_end) & (line <= moments_end + 3), 1.0, 0.0)
         mix = jnp.where(row == feats - 1, steep, mix).astype(bf16)
         across = hid // 128
-        for c in range(across):
-            sums = jnp.concatenate([sums_ref[r * across + c] for r in range(8)], axis=0)
+        for c in range(0, across, 2):
+            sums = jnp.concatenate(
+                [
+                    jnp.concatenate([sums_ref[r * across + c + d] for r in range(8)], axis=0)
+                    for d in range(2)
+                ],
+                axis=1,
+            )
             high, middle = two_parts(sums)
             low = (sums - high.astype(f32) - middle.astype(f32)).astype(bf16)
-            grad = dot(mix, high) + (dot(mix, middle) + dot(mix, low))
-            span = slice(128 * c, 128 * c + 128)
+            grad = dot(mix, jnp.concatenate([high, middle, low], axis=0))
+            span = slice(128 * c, 128 * c + 256)
             input_out_ref[:, span] = input_ref[:, span] - 2.0 * grad
 
     bias_out_ref[...] -= step * jnp.sum(value.astype(f32), axis=0, keepdims=True)
@@ -776,85 +782,6 @@
     )(turned, misfit, weight, bias, sums, input_layer)
 
 
-def update_kernel(
-    turned_ref, misfit_ref, weight_ref, bias_ref, sums_ref, input_ref,
-    next_ref, misfit_out_ref, bias_out_ref, input_out_ref,
-):
-    f32, bf16 = jnp.float32, jnp.bfloat16
-    step = 1.0 / misfit_ref.shape[0]
-    block = 256
-
-    def columns(n, none):
-        span = pl.ds(pl.multiple_of(n * block, block), block)
-        change = dot(turned_ref[...], misfit_ref[:, span])
-        next_ref[:, span] = (weight_ref[:, span].astype(f32) + change).astype(bf16)
-        return none
-
-    lax.fori_loop(0, misfit_ref.shape[1] // block, columns, 0, unroll=True)
-    rows = misfit_out_ref.shape[0]
-    here = pl.multiple_of(pl.program_id(0) * rows, rows)
-    value = misfit_ref[pl.ds(here, rows)]
-    misfit_out_ref[...] = value
-
-    @pl.when(pl.program_id(0) == 0)
-    def _():
-        bias_out_ref[...] = bias_ref[...]
-        feats, hid = input_ref.shape
-        kept = LEVELS - 1
-        levels_end, moments_end = CLASSES * kept, CLASSES * kept + STEPS - 1
-        row = lax.broadcasted_iota(jnp.int32, (feats, 64), 0)
-        line = lax.broadcasted_iota(jnp.int32, (feats, 64), 1)
-        group = jnp.where(row < CLASSES * LEVELS, row // LEVELS, CLASSES)
-        inner = row - group * LEVELS
-        length = jnp.where(group < CLASSES, kept, STEPS - 1)
-        line_group = jnp.where(line < levels_end, line // kept, CLASSES)
-        line_inner = line - line_group * kept
-        same = (group == line_group) & (line < moments_end)
-        mix = jnp.where(same & (inner == line_inner), 1.0, 0.0)
-        mix = jnp.where(inner == length, jnp.where(same, -1.0, mix), mix)
-        mix = jnp.where((inner == length) & (line == moments_end), 1.0, mix)
-        steep = jnp.where((line > moments_end) & (line <= moments_end + 3), 1.0, 0.0)
-        mix = jnp.where(row == feats - 1, steep, mix).astype(bf16)
-        across = hid // 128
-        for c in range(across):
-            sums = jnp.concatenate([sums_ref[r * across + c] for r in range(8)], axis=0)
-            high, middle = two_parts(sums)
-            low = (sums - high.astype(f32) - middle.astype(f32)).astype(bf16)
-            grad = dot(mix, high) + (dot(mix, middle) + dot(mix, low))
-            span = slice(128 * c, 128 * c + 128)
-            input_out_ref[:, span] = input_ref[:, span] - 2.0 * grad
-
-    bias_out_ref[...] -= step * jnp.sum(value.astype(f32), axis=0, keepdims=True)
-
-
-def update(turned, misfit, weight, bias, sums, input_layer):
-    hid, cells = weight.shape
-    runs = misfit.shape[0]
-    steps = 4
-    whole = pl.BlockSpec((runs, cells), lambda i: (0, 0))
-    line = pl.BlockSpec((1, cells), lambda i: (0, 0))
-    layer = pl.BlockSpec(input_layer.shape, lambda i: (0, 0))
-    all_sums = pl.BlockSpec(sums.shape, lambda i: (0, 0, 0))
-    tile = pl.BlockSpec((hid // steps, cells), lambda i: (i, 0))
-    return pl.pallas_call(
-        update_kernel,
-        grid=(steps,),
-        out_shape=(
-            jax.ShapeDtypeStruct(weight.shape, weight.dtype),
-            jax.ShapeDtypeStruct(misfit.shape, misfit.dtype),
-            jax.ShapeDtypeStruct(bias.shape, bias.dtype),
-            jax.ShapeDtypeStruct(input_layer.shape, input_layer.dtype),
-        ),
-        in_specs=[pl.BlockSpec((hid // steps, runs), lambda i: (i, 0)), whole, tile, line, all_sums, layer],
-        out_specs=(tile, pl.BlockSpec((runs // steps, cells), lambda i: (i, 0)), line, layer),
-        compiler_params=pltpu.CompilerParams(vmem_limit_bytes=60 * MIB),
-        cost_estimate=pl.CostEstimate(
-            flops=2 * hid * cells * runs, bytes_accessed=4 * hid * cells, transcendentals=0
-        ),
-        name="update",
-    )(turned, misfit, weight, bias, sums, input_layer)
-
-
 def sum_kernel(
     part_ref, out_ref, pair, own, landed, mine,
     pair_send, pair_recv, part_send, part_recv, back_send, back_recv, last_send, last_recv,

time: 113 us -> 112 us (level)
  no operation moved by 1% of the time
where the time goes in v8:
time: 112 us
  Pallas kernels  112 us (100%)
    pallas_call x1, Pallas kernels, solve(): pl.pallas_call(solve_kernel, out_shape=(jax.ShapeDtypeStruct((all_runs, c...  99.4 us
    pallas_call x1, Pallas kernels, update(): pl.pallas_call(update_kernel, grid=(steps,), out_shape=(jax.ShapeDtypeStr...  12.2 us

profile of v8, /device:TPU:1, one launch (start us, length us, event | category | flops | bytes accessed | tf_op | source)
XLA Modules:
  0.0 112.2 jit_solution(4976648621572093792)
XLA Ops:
  0.6 99.4 %solve.1 = (bf16[512,2048]{1,0:T(8,128)(2,1)}, bf16[2048,512]{1,0:T(8,128)(2,1)}, f32[128,8,128]{2,1,0:T(8,128)}) custom-call(f32[2048,512]{1,0:T(8,128)} %bitcast.6, s32[16,512]{1,0:T(8,128)} %ids_ref.1, s32[8,512]{1,0:T(8,128)} %bitcast.7, f32[1,512]{1,0:T(1,128)} %bitcast.10, s32[1,512]{1,0:T(1,128)} %bitcast.11, f32[69,2048]{1,0:T(8,128)} %input_ref.3, ...), custom_call_target="tpu_custom_call" | custom-call | tf_op jit(solution)/shard_map/solve/pallas_call | solution.py:637
  100.0 12.2 %update.1 = (bf16[2048,2048]{1,0:T(8,128)(2,1)}, bf16[512,2048]{1,0:T(8,128)(2,1)}, f32[1,2048]{1,0:T(1,128)}, f32[69,2048]{1,0:T(8,128)}) custom-call(bf16[2048,512]{1,0:T(8,128)(2,1)} %get-tuple-element.11.turned_ref, bf16[512,2048]{1,0:T(8,128)(2,1)} %get-tuple-element.12.misfit_ref, bf16[2048,2048]{1,0:T(8,128)(2,1)} %weight_ref.3, f32[1,2048]{1,0:T(1,128)} %bitcast.9, ...), custom_call_target="tpu_custom_call" | custom-call | flops 4294967296 | bytes 16777216 | tf_op jit(solution)/shard_map/update/pallas_call | solution.py:766
